TPU v7x, 32 devices: a whole 2x2x4 slice. The times are simulated.
32 devices in a mesh: dom: 32 (over z, y, x, core).
Axes of the slice: x: 2, y: 2, z: 4, core: 2. Of those that a mesh axis runs over, the one named last changes fastest.
Arguments:
- ham_core: float32 [20480, 1280], P('dom')
- halo_rows: float32 [32, 8, 80, 1280], P('dom'), as said below
- halo_request: int32 [32, 160], P('dom'), may hold values from -1 to 159, as said below
- deriv: float32 [3, 5120, 4, 1280], P(None, 'dom'), may hold values from -15 to 15
- e_low: float32 [1], replicated, may hold values from -8 to -5
- e_high: float32 [1], replicated, may hold values from 4.5 to 7.5
- branches: int32 [5], replicated, may hold values from 0 to 1
Outputs:
- density: float32 [20480, 1280], P('dom')
- forces: float32 [3, 5120], P(None, 'dom')
Inputs may be any that keep to these rules, and one draw needn't show every extreme that they name: Entry halo_request[d, k * 20 + s] is an atom index of the owner of block k of d, or -1 for an empty slot; in each block of 20 the live entries come first and are distinct; in every draw some partition asks 20 atoms of each of its 8 neighbours and is asked 20 atoms by each of them. For c < 640: halo_rows[p, k, r, c] equals ham_core[d * 640 + c, 640 + 4 * 20 * k + r] with d = (p - off_k) mod 32.
All inputs are finite; a program needn't handle non-finite values.
Results may differ from a plain program's by a relative error of at most 0.0003.
Values sent between devices are 32-bit elements; how exact they have to be, the bound alone decides.
No kernel may reach another device: no remote copies, remote signals or barrier semaphores. Data moves between devices by JAX's collectives and lax.ppermute only.
A program may use at most 128 MiB of HBM per device.

v0:
```python
import jax
import jax.numpy as jnp
from jax import lax
from jax.sharding import PartitionSpec as P

ORB = 4
ATOM_DEV = 160
NB = 4
ITERS = 5


def passed_along(value, axis, steps):
    count = lax.axis_size(axis)
    pairs = [(source, (source + steps) % count) for source in range(count)]
    return lax.ppermute(value, axis, pairs)


def product(left, right):
    return jnp.dot(left, right, precision=lax.Precision.HIGHEST, preferred_element_type=jnp.float32)


def block_offset(block):
    if block < NB:
        return block + 1
    return NB - 1 - block


def per_device(ham_core, halo_rows, halo_request, deriv, e_low, e_high, branches):
    row_count, order_all = ham_core.shape
    request = halo_request[0]
    slot_count = request.shape[0]
    block_count = 2 * NB
    per_block = slot_count // block_count
    live_halo = jnp.repeat((request >= 0).astype(jnp.float32), ORB)
    live_mask = jnp.concatenate([jnp.ones((row_count,), jnp.float32), live_halo])
    spread = e_high[0] - e_low[0]
    diagonal = jnp.diag(e_high[0] * live_mask)
    outgoing = halo_rows[0]
    core_square = None
    pieces = []
    for block in range(block_count):
        pieces.append(passed_along(outgoing[block], "dom", -block_offset(block)))
    arrived = jnp.stack(pieces, axis=0)
    whole_ham = (
        jnp.concatenate([ham_core, arrived.reshape(-1, order_all)], axis=0)
        * live_mask[:, None]
        * live_mask[None, :]
    )
    symmetric = 0.5 * (whole_ham + whole_ham.T)
    projector = (diagonal - symmetric) / spread
    for number in range(ITERS):
        square = product(projector, projector)
        projector = jnp.where(branches[number] == 1, 2.0 * projector - square, square)
    density = projector[:row_count]
    weighted = jnp.sum(density.reshape(ATOM_DEV, ORB, order_all)[None] * deriv, axis=2)
    pair_force = 2.0 * jnp.sum(weighted.reshape(3, ATOM_DEV, -1, ORB), axis=3)
    own_force = jnp.sum(pair_force, axis=2)
    reaction = -jnp.sum(pair_force, axis=1)
    halo_terms = reaction[:, ATOM_DEV:].reshape(3, block_count, per_block)
    request_block = request.reshape(block_count, per_block)
    selector = (
        request_block[:, :, None] == jnp.arange(ATOM_DEV, dtype=jnp.int32)[None, None, :]
    ).astype(jnp.float32)
    owner_terms = jnp.einsum("ckn,kna->kca", halo_terms, selector, precision=lax.Precision.HIGHEST)
    forces = own_force + reaction[:, :ATOM_DEV]
    for block in range(block_count):
        forces = forces + passed_along(owner_terms[block], "dom", block_offset(block))
    return (density, forces)


def solution(mesh):
    in_specs = (
        P("dom", None),
        P("dom", None, None, None),
        P("dom", None),
        P(None, "dom", None, None),
        P(),
        P(),
        P(),
    )
    out_specs = (P("dom", None), P(None, "dom"))
    return jax.shard_map(
        per_device, mesh=mesh, in_specs=in_specs, out_specs=out_specs, check_vma=False
    )
```

profile of v0, /device:TPU:0, one launch (start us, length us, event | category | flops | bytes accessed | tf_op | source)
XLA Modules:
  0.0 294.0 jit_solution(10046339997355965233)
XLA Ops:
  0.7 3.6 %slice_bitcast_fusion = (f32[80,1280]{1,0:T(8,128)}, f32[80,1280]{1,0:T(8,128)}, f32[80,1280]{1,0:T(8,128)}, f32[80,1280]{1,0:T(8,128)}, f32[80,1280]{1,0:T(8,12...) fusion(f32[1,8,80,1280]{3,2,1,0:T(8,128)} %param.8), kind=kLoop, calls=%fused_computation.29 | loop fusion | bytes 6553600 | tf_op jit(solution)/shard_map/squeeze | solution.py:42
  4.3 6.4 %collective-permute-start = (f32[80,1280]{1,0:T(8,128)}, f32[80,1280]{1,0:T(8,128)}, u32[]{:S(2)}, u32[]{:S(2)}) collective-permute-start(f32[80,1280]{1,0:T(8,128)} %get-tuple-element.10), channel_id=1, source_target_pairs={{0,31},{1,0},{2,1},{3,2},{4,3},{5,4},{6,5},{7,6},{8,7},{9,8},{10,9... | collective-permute-start | bytes 1228808 | tf_op jit(solution)/shard_map/ppermute | solution.py:15
  10.6 0.6 collective-permute-start.1
  11.2 0.3 collective-permute-start.2
  11.5 1.4 collective-permute-start.3
  12.9 0.9 collective-permute-start.4
  14.5 0.1 broadcast_in_dim.25
  14.6 0.1 reshape.51
  14.7 3.5 %copy.16 = f32[640,1280]{0,1:T(8,128)S(1)} copy(f32[640,1280]{1,0:T(8,128)} %param.7) | data formatting | bytes 6553600 | tf_op args[0]
  18.8 0.7 fusion.23
  22.7 0.5 broadcast.20
  23.2 0.7 reduce.3
  23.9 0.1 eq.60
  24.0 0.6 collective-permute-done
  24.6 0.0 collective-permute-start.5
  24.6 1.8 bitcast_dynamic-update-slice_fusion.7
  26.4 14.8 %collective-permute-done.1 = f32[80,1280]{1,0:T(8,128)} collective-permute-done((f32[80,1280]{1,0:T(8,128)}, f32[80,1280]{1,0:T(8,128)}, u32[]{:S(2)}, u32[]{:S(2)}) %collective-permute-start.1) | collective-permute-done | bytes 409632 | tf_op jit(solution)/shard_map/ppermute | solution.py:15
  41.2 0.0 collective-permute-start.6
  41.2 1.8 bitcast_dynamic-update-slice_fusion.6
  43.0 9.1 %collective-permute-done.2 = f32[80,1280]{1,0:T(8,128)} collective-permute-done((f32[80,1280]{1,0:T(8,128)}, f32[80,1280]{1,0:T(8,128)}, u32[]{:S(2)}, u32[]{:S(2)}) %collective-permute-start.2) | collective-permute-done | bytes 409632 | tf_op jit(solution)/shard_map/ppermute | solution.py:15
  52.1 0.0 collective-permute-start.7
  52.1 1.8 bitcast_dynamic-update-slice_fusion.5
  53.9 2.7 collective-permute-done.3
  56.6 1.8 bitcast_dynamic-update-slice_fusion.4
  58.4 0.0 collective-permute-done.4
  58.4 1.8 bitcast_dynamic-update-slice_fusion.3
  60.1 0.0 collective-permute-done.5
  60.1 0.8 bitcast_dynamic-update-slice_fusion.2
  60.9 0.8 bitcast_dynamic-update-slice_fusion.1
  61.7 5.6 %collective-permute-done.7 = f32[80,1280]{1,0:T(8,128)S(1)} collective-permute-done((f32[80,1280]{1,0:T(8,128)}, f32[80,1280]{1,0:T(8,128)S(1)}, u32[]{:S(2)}, u32[]{:S(2)}) %collective-permute-start.7) | collective-permute-done | bytes 409632 | tf_op jit(solution)/shard_map/ppermute | solution.py:15
  67.3 0.8 bitcast_dynamic-update-slice_fusion
  68.1 4.6 %copy.17 = f32[640,1280]{0,1:T(8,128)} copy(f32[640,1280]{1,0:T(8,128)} %bitcast.23) | data formatting | bytes 6553600 | tf_op jit(solution)/shard_map/reshape | solution.py:45
  72.6 4.6 %fusion = f32[1280,1280]{0,1:T(8,128)} fusion(f32[640,1280]{0,1:T(8,128)} %copy.17, f32[640,1280]{0,1:T(8,128)S(1)} %copy.16, f32[1280]{0:T(1024)S(1)} %get-tuple-element.21), kind=kLoop, calls=%fused_computation.6 | loop fusion | flops 4915200 | bytes 13112320 | tf_op jit(solution)/shard_map/mul | solution.py:45
  77.2 8.2 %copy.18 = f32[1280,1280]{1,0:T(8,128)} copy(f32[1280,1280]{0,1:T(8,128)} %fusion) | data formatting | bytes 13107200 | tf_op jit(solution)/shard_map/mul | solution.py:45
  85.4 41.6 %subtract_select_fusion.3 = f32[1280,1280]{1,0:T(8,128)S(1)} fusion(f32[1280,1280]{1,0:T(8,128)} %copy.18, f32[1280,1280]{0,1:T(8,128)} %fusion, f32[]{:T(128)S(6)} %sub.22, f32[1280]{0:T(1024)S(1)} %get-tuple-element.20, pred[]{:T(512)} %bitcast.4), kind=kOutput, calls=%fused_computation.4 | convolution fusion | flops 25190400000 | bytes 19665924 | tf_op jit(solution)/shard_map/dot_general | solution.py:19
  127.0 27.4 %subtract_select_fusion.2 = f32[1280,1280]{1,0:T(8,128)S(1)} fusion(f32[1280,1280]{1,0:T(8,128)S(1)} %subtract_select_fusion.3, pred[]{:T(512)} %bitcast.3), kind=kOutput, calls=%fused_computation.3 | convolution fusion | flops 25170739200 | bytes 13107201 | tf_op jit(solution)/shard_map/dot_general | solution.py:19
  154.5 36.0 %subtract_select_fusion.1 = f32[1280,1280]{1,0:T(8,128)S(1)} fusion(f32[1280,1280]{1,0:T(8,128)S(1)} %subtract_select_fusion.2, pred[]{:T(512)} %bitcast.2), kind=kOutput, calls=%fused_computation.2 | convolution fusion | flops 25170739200 | bytes 13107201 | tf_op jit(solution)/shard_map/dot_general | solution.py:19
  190.5 27.0 %subtract_select_fusion = f32[1280,1280]{1,0:T(8,128)S(1)} fusion(f32[1280,1280]{1,0:T(8,128)S(1)} %subtract_select_fusion.1, pred[]{:T(512)} %bitcast.1), kind=kOutput, calls=%fused_computation.1 | convolution fusion | flops 25170739200 | bytes 13107201 | tf_op jit(solution)/shard_map/dot_general | solution.py:19
  217.5 26.5 %fusion.24 = f32[1280,1280]{1,0:T(8,128)S(1)} fusion(f32[1280,1280]{1,0:T(8,128)S(1)} %subtract_select_fusion), kind=kOutput, calls=%fused_computation.63 | convolution fusion | flops 25165824000 | bytes 13107200 | tf_op jit(solution)/shard_map/dot_general | solution.py:19
  244.1 0.4 subtract_select_fusion.4
  244.5 0.0 copy-start
  244.5 2.7 mul.72
  247.2 10.8 %multiply_reduce_fusion = f32[3,160,1280]{2,1,0:T(8,128)} fusion(f32[3,160,4,1280]{3,2,1,0:T(4,128)} %param.10, f32[160,4,1280]{2,1,0:T(4,128)} %mul.72), kind=kLoop, calls=%fused_computation | loop fusion | flops 4300800 | bytes 15564800 | tf_op jit(solution)/shard_map/reduce_sum | solution.py:55
  258.0 4.8 %copy.19 = f32[3,160,1280]{1,2,0:T(8,128)} copy(f32[3,160,1280]{2,1,0:T(8,128)} %multiply_reduce_fusion) | data formatting | bytes 4915200 | tf_op jit(solution)/shard_map/reduce_sum | solution.py:55
  262.7 5.1 %reshape.53 = f32[3,160,320,4]{1,3,2,0:T(4,128)} reshape(f32[3,160,1280]{1,2,0:T(8,128)} %copy.19) | data formatting | bytes 4915200 | tf_op jit(solution)/shard_map/reshape | solution.py:56
  267.9 4.5 %reduce_sum.37 = f32[3,160,320]{1,2,0:T(8,128)S(1)} reduce(f32[3,160,320,4]{1,3,2,0:T(4,128)} %reshape.53, f32[]{:T(128)} %constant.17.clone.1), dimensions={3}, to_apply=%region_1.2 | reduce | flops 460800 | bytes 3072004 | tf_op jit(solution)/shard_map/reduce_sum | solution.py:56
  272.4 0.3 multiply_reduce_fusion.2
  272.6 0.1 slice.107
  272.7 0.1 reshape.54
  272.8 0.3 fusion.10
  273.1 0.1 collective-permute-start.10
  273.1 0.7 collective-permute-start.11
  273.9 0.2 collective-permute-start.12
  274.1 8.5 %collective-permute-start.13 = (f32[3,160]{1,0:T(4,128)S(1)}, f32[3,160]{1,0:T(4,128)S(1)}, u32[]{:S(2)}, u32[]{:S(2)}) collective-permute-start(f32[3,160]{1,0:T(4,128)S(1)} %get-tuple-element.15), channel_id=1, source_target_pairs={{0,30},{1,31},{2,0},{3,1},{4,2},{5,3},{6,4},{7,5},{8,6},{9,7},{10,... | collective-permute-start | bytes 5768 | tf_op jit(solution)/shard_map/ppermute | solution.py:15
  282.6 0.4 collective-permute-start.14
  282.9 0.0 collective-permute-done.10
  282.9 2.9 collective-permute-start.15
  285.9 0.1 collective-permute-start.9
  285.9 0.0 collective-permute-done.13
  285.9 0.0 collective-permute-done.14
  286.0 1.2 collective-permute-done.15
  287.2 5.3 %collective-permute-done.8 = f32[3,160]{1,0:T(4,128)S(1)} collective-permute-done((f32[3,160]{1,0:T(4,128)S(1)}, f32[3,160]{1,0:T(4,128)S(1)}, u32[]{:S(2)}, u32[]{:S(2)}) %collective-permute-start.8) | collective-permute-done | bytes 1952 | tf_op jit(solution)/shard_map/ppermute | solution.py:15
  292.5 0.6 collective-permute-done.9
  293.1 0.6 fusion.20
  (13 shorter events, 0.0 us)
Async XLA Ops:
  0.6 13.9 %copy-start.2 = (s32[1,160]{1,0:T(1,128)S(1)}, s32[1,160]{1,0:T(1,128)}, u32[]{:S(2)}) copy-start(s32[1,160]{1,0:T(1,128)} %param.9) | copy-start | bytes 1924
  0.6 18.2 %copy-start.1 = (s32[5]{0:T(128)S(1)}, s32[5]{0:T(128)}, u32[]{:S(2)}) copy-start(s32[5]{0:T(128)} %param.13) | copy-start | bytes 64
  4.3 20.4 %collective-permute-start = (f32[80,1280]{1,0:T(8,128)}, f32[80,1280]{1,0:T(8,128)}, u32[]{:S(2)}, u32[]{:S(2)}) collective-permute-start(f32[80,1280]{1,0:T(8,128)} %get-tuple-element.10), channel_id=1, source_target_pairs={{0,31},{1,0},{2,1},{3,2},{4,3},{5,4},{6,5},{7,6},{8,7},{9,8},{10,9... | collective-permute-start | bytes 1228808 | tf_op jit(solution)/shard_map/ppermute | solution.py:15
  10.6 30.6 %collective-permute-start.1 = (f32[80,1280]{1,0:T(8,128)}, f32[80,1280]{1,0:T(8,128)}, u32[]{:S(2)}, u32[]{:S(2)}) collective-permute-start(f32[80,1280]{1,0:T(8,128)} %get-tuple-element.9), channel_id=1, source_target_pairs={{0,30},{1,31},{2,0},{3,1},{4,2},{5,3},{6,4},{7,5},{8,6},{9,7},{10,... | collective-permute-start | bytes 1228808 | tf_op jit(solution)/shard_map/ppermute | solution.py:15
  11.2 40.8 %collective-permute-start.2 = (f32[80,1280]{1,0:T(8,128)}, f32[80,1280]{1,0:T(8,128)}, u32[]{:S(2)}, u32[]{:S(2)}) collective-permute-start(f32[80,1280]{1,0:T(8,128)} %get-tuple-element.8), channel_id=1, source_target_pairs={{0,29},{1,30},{2,31},{3,0},{4,1},{5,2},{6,3},{7,4},{8,5},{9,6},{10... | collective-permute-start | bytes 1228808 | tf_op jit(solution)/shard_map/ppermute | solution.py:15
  11.5 45.1 %collective-permute-start.3 = (f32[80,1280]{1,0:T(8,128)}, f32[80,1280]{1,0:T(8,128)}, u32[]{:S(2)}, u32[]{:S(2)}) collective-permute-start(f32[80,1280]{1,0:T(8,128)} %get-tuple-element.7), channel_id=1, source_target_pairs={{0,28},{1,29},{2,30},{3,31},{4,0},{5,1},{6,2},{7,3},{8,4},{9,5},{1... | collective-permute-start | bytes 1228808 | tf_op jit(solution)/shard_map/ppermute | solution.py:15
  12.9 45.4 %collective-permute-start.4 = (f32[80,1280]{1,0:T(8,128)}, f32[80,1280]{1,0:T(8,128)}, u32[]{:S(2)}, u32[]{:S(2)}) collective-permute-start(f32[80,1280]{1,0:T(8,128)} %get-tuple-element.6), channel_id=1, source_target_pairs={{0,1},{1,2},{2,3},{3,4},{4,5},{5,6},{6,7},{7,8},{8,9},{9,10},{10,1... | collective-permute-start | bytes 1228808 | tf_op jit(solution)/shard_map/ppermute | solution.py:15
  24.6 35.5 %collective-permute-start.5 = (f32[80,1280]{1,0:T(8,128)}, f32[80,1280]{1,0:T(8,128)S(1)}, u32[]{:S(2)}, u32[]{:S(2)}) collective-permute-start(f32[80,1280]{1,0:T(8,128)} %get-tuple-element.5), channel_id=1, source_target_pairs={{0,2},{1,3},{2,4},{3,5},{4,6},{5,7},{6,8},{7,9},{8,10},{9,11},{10,... | collective-permute-start | bytes 1228808 | tf_op jit(solution)/shard_map/ppermute | solution.py:15
  41.2 19.7 %collective-permute-start.6 = (f32[80,1280]{1,0:T(8,128)}, f32[80,1280]{1,0:T(8,128)S(1)}, u32[]{:S(2)}, u32[]{:S(2)}) collective-permute-start(f32[80,1280]{1,0:T(8,128)} %get-tuple-element.11), channel_id=1, source_target_pairs={{0,3},{1,4},{2,5},{3,6},{4,7},{5,8},{6,9},{7,10},{8,11},{9,12},{10... | collective-permute-start | bytes 1228808 | tf_op jit(solution)/shard_map/ppermute | solution.py:15
  52.1 15.2 %collective-permute-start.7 = (f32[80,1280]{1,0:T(8,128)}, f32[80,1280]{1,0:T(8,128)S(1)}, u32[]{:S(2)}, u32[]{:S(2)}) collective-permute-start(f32[80,1280]{1,0:T(8,128)} %get-tuple-element.4), channel_id=1, source_target_pairs={{0,4},{1,5},{2,6},{3,7},{4,8},{5,9},{6,10},{7,11},{8,12},{9,13},{1... | collective-permute-start | bytes 1228808 | tf_op jit(solution)/shard_map/ppermute | solution.py:15
  244.5 13.5 %copy-start = (f32[640,1280]{1,0:T(8,128)}, f32[640,1280]{1,0:T(8,128)S(1)}, u32[]{:S(2)}) copy-start(f32[640,1280]{1,0:T(8,128)S(1)} %subtract_select_fusion.4) | copy-start | bytes 9830404
  273.1 9.9 %collective-permute-start.10 = (f32[3,160]{1,0:T(4,128)S(1)}, f32[3,160]{1,0:T(4,128)S(1)}, u32[]{:S(2)}, u32[]{:S(2)}) collective-permute-start(f32[3,160]{1,0:T(4,128)S(1)} %get-tuple-element.18), channel_id=1, source_target_pairs={{0,3},{1,4},{2,5},{3,6},{4,7},{5,8},{6,9},{7,10},{8,11},{9,12},{10... | collective-permute-start | bytes 5768 | tf_op jit(solution)/shard_map/ppermute | solution.py:15
  273.1 12.7 %collective-permute-start.11 = (f32[3,160]{1,0:T(4,128)S(1)}, f32[3,160]{1,0:T(4,128)S(1)}, u32[]{:S(2)}, u32[]{:S(2)}) collective-permute-start(f32[3,160]{1,0:T(4,128)S(1)} %get-tuple-element.17), channel_id=1, source_target_pairs={{0,4},{1,5},{2,6},{3,7},{4,8},{5,9},{6,10},{7,11},{8,12},{9,13},{1... | collective-permute-start | bytes 5768 | tf_op jit(solution)/shard_map/ppermute | solution.py:15
  273.9 12.0 %collective-permute-start.12 = (f32[3,160]{1,0:T(4,128)S(1)}, f32[3,160]{1,0:T(4,128)S(1)}, u32[]{:S(2)}, u32[]{:S(2)}) collective-permute-start(f32[3,160]{1,0:T(4,128)S(1)} %get-tuple-element.16), channel_id=1, source_target_pairs={{0,31},{1,0},{2,1},{3,2},{4,3},{5,4},{6,5},{7,6},{8,7},{9,8},{10,9... | collective-permute-start | bytes 5768 | tf_op jit(solution)/shard_map/ppermute | solution.py:15
  274.1 11.9 %collective-permute-start.13 = (f32[3,160]{1,0:T(4,128)S(1)}, f32[3,160]{1,0:T(4,128)S(1)}, u32[]{:S(2)}, u32[]{:S(2)}) collective-permute-start(f32[3,160]{1,0:T(4,128)S(1)} %get-tuple-element.15), channel_id=1, source_target_pairs={{0,30},{1,31},{2,0},{3,1},{4,2},{5,3},{6,4},{7,5},{8,6},{9,7},{10,... | collective-permute-start | bytes 5768 | tf_op jit(solution)/shard_map/ppermute | solution.py:15
  282.6 3.4 %collective-permute-start.14 = (f32[3,160]{1,0:T(4,128)S(1)}, f32[3,160]{1,0:T(4,128)S(1)}, u32[]{:S(2)}, u32[]{:S(2)}) collective-permute-start(f32[3,160]{1,0:T(4,128)S(1)} %get-tuple-element.14), channel_id=1, source_target_pairs={{0,29},{1,30},{2,31},{3,0},{4,1},{5,2},{6,3},{7,4},{8,5},{9,6},{10... | collective-permute-start | bytes 5768 | tf_op jit(solution)/shard_map/ppermute | solution.py:15
  282.9 4.3 %collective-permute-start.15 = (f32[3,160]{1,0:T(4,128)S(1)}, f32[3,160]{1,0:T(4,128)S(1)}, u32[]{:S(2)}, u32[]{:S(2)}) collective-permute-start(f32[3,160]{1,0:T(4,128)S(1)} %get-tuple-element.13), channel_id=1, source_target_pairs={{0,28},{1,29},{2,30},{3,31},{4,0},{5,1},{6,2},{7,3},{8,4},{9,5},{1... | collective-permute-start | bytes 5768 | tf_op jit(solution)/shard_map/ppermute | solution.py:15
  285.9 6.6 %collective-permute-start.8 = (f32[3,160]{1,0:T(4,128)S(1)}, f32[3,160]{1,0:T(4,128)S(1)}, u32[]{:S(2)}, u32[]{:S(2)}) collective-permute-start(f32[3,160]{1,0:T(4,128)S(1)} %get-tuple-element.12), channel_id=1, source_target_pairs={{0,1},{1,2},{2,3},{3,4},{4,5},{5,6},{6,7},{7,8},{8,9},{9,10},{10,1... | collective-permute-start | bytes 5768 | tf_op jit(solution)/shard_map/ppermute | solution.py:15
  285.9 7.3 %collective-permute-start.9 = (f32[3,160]{1,0:T(4,128)S(1)}, f32[3,160]{1,0:T(4,128)S(1)}, u32[]{:S(2)}, u32[]{:S(2)}) collective-permute-start(f32[3,160]{1,0:T(4,128)S(1)} %get-tuple-element.19), channel_id=1, source_target_pairs={{0,2},{1,3},{2,4},{3,5},{4,6},{5,7},{6,8},{7,9},{8,10},{9,11},{10,... | collective-permute-start | bytes 5768 | tf_op jit(solution)/shard_map/ppermute | solution.py:15
where the time goes:
time: 298 us; the launch traced here: 294 us
  matrix products  159 us (53%)
  local copies, waits for them, and re-layouts  45.2 us (15%)
  waiting for transfers between devices  40 us (13%)
  starting transfers between devices  22.4 us (8%)
  other arithmetic  21.9 us (7%)
  between operations  5.55 us (2%)
    dot_general x5, matrix products, product(): jnp.dot(left, right, precision=lax.Precision.HIGHEST, preferred_element_t...  159 us
    ppermute x16, waiting for transfers between devices, passed_along(): return lax.ppermute(value, axis, pairs)  40 us
    ppermute x16, starting transfers between devices, passed_along(): return lax.ppermute(value, axis, pairs)  22.4 us
    unnamed x15, local copies, waits for them, and re-layouts  14.5 us
    reduce_sum x1, other arithmetic, per_device(): jnp.sum(density.reshape(ATOM_DEV, ORB, order_all)[None] * deriv, axis=2)  10.8 us
    mul x1, local copies, waits for them, and re-layouts, per_device(): jnp.concatenate([ham_core, arrived.reshape(-1, order_all)], axis=0)  8.17 us
  transfers between devices with their start and end apart: 16, of which 8 were waited for; matrix products, arithmetic and copies ran while one was open for 5% of the time, Pallas kernels for 0%

commit v1 on v0

v1 whole, which is shorter than its diff:
```python
import functools

import jax
import jax.numpy as jnp
from jax import lax
from jax.experimental import pallas as pl
from jax.experimental.pallas import tpu as pltpu
from jax.sharding import PartitionSpec as P

ORB = 4
NB = 4
ITERS = 5
PANEL = 256
SUB = 128
VMEM_BYTES = 56 * 1024 * 1024


def passed_along(value, axis, steps):
    count = lax.axis_size(axis)
    pairs = [(source, (source + steps) % count) for source in range(count)]
    return lax.ppermute(value, axis, pairs)


def block_offset(block):
    if block < NB:
        return block + 1
    return NB - 1 - block


def halves(value):
    high = value.astype(jnp.bfloat16)
    low = (value - high.astype(jnp.float32)).astype(jnp.bfloat16)
    return high, low


def thirds(value):
    high = value.astype(jnp.bfloat16)
    rest = value - high.astype(jnp.float32)
    middle, low = halves(rest)
    return high, middle, low


def dot(left, right):
    return jnp.dot(left, right, preferred_element_type=jnp.float32)


def dot_one_hot(value, one_hot):
    return sum(dot(part, one_hot) for part in thirds(value))


def kernel(
    ends, branches, core, request_row, request_col, deriv, *refs
):
    block_count = 2 * NB
    pieces = refs[:block_count]
    density_out, own_out = refs[block_count : block_count + 2]
    halo_outs = refs[block_count + 2 : 2 * block_count + 2]
    (x, high_a, low_a, high_b, low_b, halo, density, deriv_held, row_part, deriv_sems, out_sem) = refs[
        2 * block_count + 2 :
    ]
    rows, order = core.shape
    atoms = rows // ORB
    slot_rows = (order - rows) // block_count

    deriv_copies = [
        pltpu.make_async_copy(deriv.at[c], deriv_held.at[c], deriv_sems.at[c]) for c in range(3)
    ]
    for copy in deriv_copies:
        copy.start()

    top = ends[0]
    scale = 1.0 / (ends[0] - ends[1])
    for block in range(block_count):
        halo[block * slot_rows : (block + 1) * slot_rows, :] = pieces[block][...]
    live_row = (request_row[...] >= 0).astype(jnp.float32)
    live_col = (request_col[...] >= 0).astype(jnp.float32)
    eye = (
        lax.broadcasted_iota(jnp.int32, (SUB, SUB), 0) == lax.broadcasted_iota(jnp.int32, (SUB, SUB), 1)
    ).astype(jnp.float32)

    def put(value, row, col):
        x[row : row + SUB, col : col + SUB] = value
        high, low = halves(value)
        high_a[row : row + SUB, col : col + SUB] = high
        low_a[row : row + SUB, col : col + SUB] = low
        if row != col:
            if row // PANEL == col // PANEL:
                x[col : col + SUB, row : row + SUB] = value.T
            high_a[col : col + SUB, row : row + SUB] = high.T
            low_a[col : col + SUB, row : row + SUB] = low.T

    for row in range(0, rows, SUB):
        for col in range(row, rows, SUB):
            value = 0.5 * (
                core[row : row + SUB, col : col + SUB] + core[col : col + SUB, row : row + SUB].T
            )
            if row == col:
                value = value - top * eye
            put(-scale * value, row, col)
    for row in range(0, rows, SUB):
        for col in range(rows, order, SUB):
            value = core[row : row + SUB, col : col + SUB] * live_row[:, col - rows : col - rows + SUB]
            put(-scale * value, row, col)
    for row in range(0, order - rows, SUB):
        for col in range(row, order - rows, SUB):
            value = 0.5 * (
                halo[row : row + SUB, col : col + SUB] + halo[col : col + SUB, row : row + SUB].T
            )
            if row == col:
                value = value - top * eye
            value = value * live_col[row : row + SUB, :] * live_row[:, col : col + SUB]
            put(-scale * value, row + rows, col + rows)

    def product(high, low, upto, cols):
        right_high, right_low = high[:, cols], low[:, cols]
        left_high, left_low = high[0:upto, :], low[0:upto, :]
        return dot(left_high, right_high) + (dot(left_high, right_low) + dot(left_low, right_high))

    def factors(number):
        taken = (branches[number] == 1).astype(jnp.float32)
        return 2.0 * taken, 1.0 - 2.0 * taken

    def squaring(number, high, low, next_high, next_low):
        keep, add = factors(number)
        for start in range(0, order, PANEL):
            end = start + PANEL
            cols = slice(start, end)
            value = keep * x[0:end, cols] + add * product(high, low, end, cols)
            x[0:end, cols] = value
            new_high, new_low = halves(value)
            next_high[0:end, cols] = new_high
            next_low[0:end, cols] = new_low
            if start > 0:
                next_high[cols, 0:start] = new_high[0:start].T
                next_low[cols, 0:start] = new_low[0:start].T

    def two(pair, carry):
        squaring(2 * pair, high_a, low_a, high_b, low_b)
        squaring(2 * pair + 1, high_b, low_b, high_a, low_a)
        return carry

    lax.fori_loop(0, (ITERS - 1) // 2, two, 0)
    keep, add = factors(ITERS - 1)
    for start in range(0, order, PANEL):
        upto = min(start + PANEL, rows)
        cols = slice(start, start + PANEL)
        value = keep * x[0:upto, cols] + add * product(high_a, low_a, upto, cols)
        density[0:upto, cols] = value
        if 0 < start < rows:
            end = min(start + PANEL, rows)
            density[start:end, 0:start] = value[0:start, 0 : end - start].T

    out_copy = pltpu.make_async_copy(density, density_out, out_sem)
    out_copy.start()

    chunk = 64
    line = lax.broadcasted_iota(jnp.int32, (8, order), 0)
    columns = jnp.zeros((8, order), jnp.float32)
    own_rows = jnp.zeros((8, rows), jnp.float32)
    ones = jnp.ones((8, SUB), jnp.bfloat16)
    for c in range(3):
        deriv_copies[c].wait()

        def strip(number, total, c=c):
            at = pl.ds(pl.multiple_of(number * chunk, chunk), chunk)
            weighted = density[at, :] * deriv_held[c, at, :]
            row_part[at, :] = sum(weighted[:, lane : lane + SUB] for lane in range(0, order, SUB))
            return total + jnp.sum(weighted.reshape(chunk // 8, 8, order), axis=0)

        total = lax.fori_loop(0, rows // chunk, strip, jnp.zeros((8, order), jnp.float32))
        columns = jnp.where(line == c, jnp.sum(total, axis=0, keepdims=True), columns)
        row_sums = sum(
            lax.dot_general(ones, part, (((1,), (1,)), ((), ())), preferred_element_type=jnp.float32)
            for part in thirds(row_part[...])
        )
        own_rows = jnp.where(line[:, :rows] == c, row_sums, own_rows)
    atom_ids = lax.broadcasted_iota(jnp.int32, (rows, atoms), 1)
    own_hot = (lax.broadcasted_iota(jnp.int32, (rows, atoms), 0) // ORB == atom_ids).astype(jnp.float32)
    own_out[...] = dot_one_hot(2.0 * (own_rows - columns[:, :rows]), own_hot.astype(jnp.bfloat16))
    asked_hot = (request_col[...] == atom_ids).astype(jnp.float32).astype(jnp.bfloat16)
    lane_block = lax.broadcasted_iota(jnp.int32, (8, order - rows), 1) // slot_rows
    halo_columns = -2.0 * columns[:, rows:]
    spread = jnp.concatenate(
        [jnp.where(lane_block == block, halo_columns, 0.0) for block in range(block_count)], axis=0
    )
    terms = dot_one_hot(spread, asked_hot)
    for block in range(block_count):
        halo_outs[block][...] = terms[8 * block : 8 * block + 8, :]
    out_copy.wait()


def density_and_terms(ends, branches, core, request_row, request_col, deriv, pieces):
    rows, order = core.shape
    atoms = rows // ORB
    block_count = len(pieces)
    vmem = pl.BlockSpec(memory_space=pltpu.VMEM)
    smem = pl.BlockSpec(memory_space=pltpu.SMEM)
    anywhere = pl.BlockSpec(memory_space=pl.ANY)
    square = (order, order)
    small = jax.ShapeDtypeStruct((8, atoms), jnp.float32)
    return pl.pallas_call(
        kernel,
        out_shape=[jax.ShapeDtypeStruct((rows, order), jnp.float32)] + [small] * (block_count + 1),
        in_specs=[smem, smem, vmem, vmem, vmem, anywhere] + [vmem] * block_count,
        out_specs=[anywhere] + [vmem] * (block_count + 1),
        scratch_shapes=[
            pltpu.VMEM(square, jnp.float32),
            pltpu.VMEM(square, jnp.bfloat16),
            pltpu.VMEM(square, jnp.bfloat16),
            pltpu.VMEM(square, jnp.bfloat16),
            pltpu.VMEM(square, jnp.bfloat16),
            pltpu.VMEM((order - rows, order - rows), jnp.float32),
            pltpu.VMEM((rows, order), jnp.float32),
            pltpu.VMEM((3, rows, order), jnp.float32),
            pltpu.VMEM((rows, SUB), jnp.float32),
            pltpu.SemaphoreType.DMA((3,)),
            pltpu.SemaphoreType.DMA,
        ],
        compiler_params=pltpu.CompilerParams(vmem_limit_bytes=VMEM_BYTES),
        cost_estimate=pl.CostEstimate(
            flops=2 * 3 * 3 * order**3, bytes_accessed=24_000_000, transcendentals=0
        ),
    )(ends, branches, core, request_row, request_col, deriv, *pieces)


def per_device(ham_core, halo_rows, halo_request, deriv, e_low, e_high, branches):
    row_count, order_all = ham_core.shape
    block_count = 2 * NB
    pieces = [
        passed_along(halo_rows[0, block, :, row_count:], "dom", -block_offset(block))
        for block in range(block_count)
    ]
    request = jnp.repeat(halo_request[0], ORB)
    outs = density_and_terms(
        jnp.concatenate([e_high, e_low]),
        branches,
        ham_core,
        request[None, :],
        request[:, None],
        deriv.reshape(3, row_count, order_all),
        pieces,
    )
    density, forces = outs[:2]
    for block in range(block_count):
        forces = forces + passed_along(outs[2 + block], "dom", block_offset(block))
    return (density, forces[:3])


def solution(mesh):
    in_specs = (
        P("dom", None),
        P("dom", None, None, None),
        P("dom", None),
        P(None, "dom", None, None),
        P(),
        P(),
        P(),
    )
    out_specs = (P("dom", None), P(None, "dom"))
    return jax.shard_map(
        per_device, mesh=mesh, in_specs=in_specs, out_specs=out_specs, check_vma=False
    )
```

time: 298 us -> 107 us (0.36); the launches traced: 294 us -> 107 us
  matrix products: 159 us -> 0 us
  Pallas kernels: 0 us -> 47.8 us
  local copies, waits for them, and re-layouts: 45.2 us -> 17 us
  waiting for transfers between devices: 40 us -> 13.8 us
  other arithmetic: 21.9 us -> 1.89 us
  between operations: 5.55 us -> 2.08 us
    dot_general x6 -> x0, matrix products: 159 us -> none  [the longest x5 159 us: product(): jnp.dot(left, right, precision=lax.Precision.HIGHEST, preferred_element_t...]
    pallas_call x0 -> x1, Pallas kernels: none -> 47.8 us  [density_and_terms(): pl.pallas_call(kernel, out_shape=[jax.ShapeDtypeStruct((rows, order), jnp...]
    ppermute x16, waiting for transfers between devices: 40 us -> 13.8 us  [passed_along(): return lax.ppermute(value, axis, pairs)]
    reduce_sum x3 -> x0, other arithmetic: 15.6 us -> none  [the longest x1 10.8 us: per_device(): jnp.sum(density.reshape(ATOM_DEV, ORB, order_all)[None] * deriv, axis=2)]
    unnamed x15 -> x18, local copies, waits for them, and re-layouts: 14.5 us -> 1.53 us
    mul x2 -> x0, local copies, waits for them, and re-layouts: 10.9 us -> none  [the longest x1 8.17 us: per_device(): jnp.concatenate([ham_core, arrived.reshape(-1, order_all)], axis=0)]
    reduce_sum x1 -> x0, local copies, waits for them, and re-layouts: 4.76 us -> none  [per_device(): jnp.sum(density.reshape(ATOM_DEV, ORB, order_all)[None] * deriv, axis=2)]
    mul x2 -> x0, other arithmetic: 4.61 us -> none  [the longest x1 4.6 us: per_device(): jnp.concatenate([ham_core, arrived.reshape(-1, order_all)], axis=0)]
  transfers between devices with their start and end apart: 16 -> 16, of which waited for: 8 -> 4; matrix products, arithmetic and copies ran while one was open for 5% -> 14% of each run, Pallas kernels for 0% -> 0%
where the time goes in v1:
time: 107 us
  Pallas kernels  47.8 us (45%)
  starting transfers between devices  24.3 us (23%)
  local copies, waits for them, and re-layouts  17 us (16%)
  waiting for transfers between devices  13.8 us (13%)
  between operations  2.08 us (2%)
  other arithmetic  1.89 us (2%)
    pallas_call x1, Pallas kernels, density_and_terms(): pl.pallas_call(kernel, out_shape=[jax.ShapeDtypeStruct((rows, order), jnp...  47.8 us
    ppermute x16, starting transfers between devices, passed_along(): return lax.ppermute(value, axis, pairs)  24.3 us
    ppermute x16, waiting for transfers between devices, passed_along(): return lax.ppermute(value, axis, pairs)  13.8 us
    reshape x1, local copies, waits for them, and re-layouts, per_device(): deriv.reshape(3, row_count, order_all)  12.3 us
  transfers between devices with their start and end apart: 16, of which 4 were waited for; matrix products, arithmetic and copies ran while one was open for 14% of the time, Pallas kernels for 0%

profile of v1, /device:TPU:0, one launch (start us, length us, event | category | flops | bytes accessed | tf_op | source)
XLA Modules:
  0.0 106.8 jit_solution(13830757048934238899)
XLA Ops:
  0.6 0.0 copy-start
  0.6 1.6 %slice_bitcast_fusion = (f32[80,640]{1,0:T(8,128)S(1)}, f32[80,640]{1,0:T(8,128)S(1)}, f32[80,640]{1,0:T(8,128)S(1)}, f32[80,640]{1,0:T(8,128)S(1)}, f32[80,640]...) fusion(f32[1,8,80,1280]{3,2,1,0:T(8,128)} %param.8), kind=kLoop, calls=%fused_computation | loop fusion | bytes 3276800 | tf_op jit(solution)/shard_map/squeeze | solution.py:230
  2.2 3.0 %collective-permute-start.7 = (f32[80,640]{1,0:T(8,128)S(1)}, f32[80,640]{1,0:T(8,128)S(1)}, u32[]{:S(2)}, u32[]{:S(2)}) collective-permute-start(f32[80,640]{1,0:T(8,128)S(1)} %get-tuple-element.22), channel_id=1, source_target_pairs={{0,4},{1,5},{2,6},{3,7},{4,8},{5,9},{6,10},{7,11},{8,12},{9,13},{1... | collective-permute-start | bytes 614408 | tf_op jit(solution)/shard_map/ppermute | solution.py:21
  5.3 1.5 %collective-permute-start.5 = (f32[80,640]{1,0:T(8,128)S(1)}, f32[80,640]{1,0:T(8,128)S(1)}, u32[]{:S(2)}, u32[]{:S(2)}) collective-permute-start(f32[80,640]{1,0:T(8,128)S(1)} %get-tuple-element.23), channel_id=1, source_target_pairs={{0,2},{1,3},{2,4},{3,5},{4,6},{5,7},{6,8},{7,9},{8,10},{9,11},{10,... | collective-permute-start | bytes 614408 | tf_op jit(solution)/shard_map/ppermute | solution.py:21
  6.7 0.0 collective-permute-start.4
  6.8 3.2 %collective-permute-start.3 = (f32[80,640]{1,0:T(8,128)S(1)}, f32[80,640]{1,0:T(8,128)S(1)}, u32[]{:S(2)}, u32[]{:S(2)}) collective-permute-start(f32[80,640]{1,0:T(8,128)S(1)} %get-tuple-element.25), channel_id=1, source_target_pairs={{0,28},{1,29},{2,30},{3,31},{4,0},{5,1},{6,2},{7,3},{8,4},{9,5},{1... | collective-permute-start | bytes 614408 | tf_op jit(solution)/shard_map/ppermute | solution.py:21
  10.0 1.3 %collective-permute-start.2 = (f32[80,640]{1,0:T(8,128)S(1)}, f32[80,640]{1,0:T(8,128)S(1)}, u32[]{:S(2)}, u32[]{:S(2)}) collective-permute-start(f32[80,640]{1,0:T(8,128)S(1)} %get-tuple-element.26), channel_id=1, source_target_pairs={{0,29},{1,30},{2,31},{3,0},{4,1},{5,2},{6,3},{7,4},{8,5},{9,6},{10... | collective-permute-start | bytes 614408 | tf_op jit(solution)/shard_map/ppermute | solution.py:21
  11.3 11.5 %collective-permute-done.7.refs_7_ = f32[80,640]{1,0:T(8,128)S(1)} collective-permute-done((f32[80,640]{1,0:T(8,128)S(1)}, f32[80,640]{1,0:T(8,128)S(1)}, u32[]{:S(2)}, u32[]{:S(2)}) %collective-permute-start.7) | collective-permute-done | bytes 204832 | tf_op jit(solution)/shard_map/ppermute | solution.py:21
  22.8 0.0 copy-start.1
  22.8 0.0 collective-permute-start.1
  22.8 0.0 collective-permute-done.5.refs_5_
  22.8 0.0 copy-start.2
  22.8 5.3 %collective-permute-start = (f32[80,640]{1,0:T(8,128)S(1)}, f32[80,640]{1,0:T(8,128)S(1)}, u32[]{:S(2)}, u32[]{:S(2)}) collective-permute-start(f32[80,640]{1,0:T(8,128)S(1)} %get-tuple-element.28), channel_id=1, source_target_pairs={{0,31},{1,0},{2,1},{3,2},{4,3},{5,4},{6,5},{7,6},{8,7},{9,8},{10,9... | collective-permute-start | bytes 614408 | tf_op jit(solution)/shard_map/ppermute | solution.py:21
  28.1 0.0 collective-permute-done.4.refs_4_
  28.1 0.0 copy-start.3
  28.1 0.0 collective-permute-start.6
  28.1 0.0 copy-done
  28.1 0.1 broadcast_in_dim.3
  28.2 0.7 broadcast_in_dim_reshape.6.request_row
  28.9 0.9 broadcast_in_dim_reshape.8.request_col
  31.1 12.3 %reshape.7.deriv = f32[3,640,1280]{2,1,0:T(8,128)} reshape(f32[3,160,4,1280]{3,2,1,0:T(4,128)} %param.10) | data formatting | bytes 19660800 | tf_op jit(solution)/shard_map/reshape | solution.py:240
  43.3 0.0 copy-done.1
  43.3 0.0 copy-done.2
  43.3 0.0 copy-done.3
  43.4 0.6 pad_maximum_fusion.ends
  43.9 0.0 collective-permute-done.3.refs_3_
  44.0 0.0 copy-start.4
  44.0 0.0 collective-permute-done.2.refs_2_
  44.0 0.0 copy-start.5
  44.0 0.0 collective-permute-done.1.refs_1_
  44.0 0.0 copy-start.6
  44.0 0.0 collective-permute-done.refs_0_
  44.0 0.0 copy-start.7
  44.0 0.0 collective-permute-done.6.refs_6_
  44.0 0.6 copy-done.4
  44.6 0.1 copy-done.5
  44.7 0.1 copy-done.6
  44.8 0.1 copy-done.7
  44.8 0.0 copy-start.8
  44.8 0.7 copy-done.8
  45.5 47.8 %shard_map.86 = (f32[640,1280]{1,0:T(8,128)}, f32[8,160]{1,0:T(8,128)}, f32[8,160]{1,0:T(8,128)}, f32[8,160]{1,0:T(8,128)}, f32[8,160]{1,0:T(8,128)}, /*index=5*...) custom-call(f32[2]{0:T(128)} %pad_maximum_fusion.ends, s32[5]{0:T(128)} %branches.1, ...), custom_call_target="tpu_custom_call" | custom-call | flops 37748736000 | bytes 24000000 | tf_op jit(solution)/shard_map/pallas_call | solution.py:201
  93.3 0.1 collective-permute-start.8
  93.4 0.1 collective-permute-start.9
  93.4 0.4 collective-permute-start.10
  93.8 2.2 %collective-permute-start.11 = (f32[8,160]{1,0:T(8,128)}, f32[8,160]{1,0:T(8,128)S(1)}, u32[]{:S(2)}, u32[]{:S(2)}) collective-permute-start(f32[8,160]{1,0:T(8,128)} %get-tuple-element.17), channel_id=1, source_target_pairs={{0,4},{1,5},{2,6},{3,7},{4,8},{5,9},{6,10},{7,11},{8,12},{9,13},{1... | collective-permute-start | bytes 15368 | tf_op jit(solution)/shard_map/ppermute | solution.py:21
  96.1 2.8 %collective-permute-start.12 = (f32[8,160]{1,0:T(8,128)}, f32[8,160]{1,0:T(8,128)S(1)}, u32[]{:S(2)}, u32[]{:S(2)}) collective-permute-start(f32[8,160]{1,0:T(8,128)} %get-tuple-element.18), channel_id=1, source_target_pairs={{0,31},{1,0},{2,1},{3,2},{4,3},{5,4},{6,5},{7,6},{8,7},{9,8},{10,9... | collective-permute-start | bytes 15368 | tf_op jit(solution)/shard_map/ppermute | solution.py:21
  98.8 1.4 %collective-permute-done.8 = f32[8,160]{1,0:T(8,128)S(1)} collective-permute-done((f32[8,160]{1,0:T(8,128)}, f32[8,160]{1,0:T(8,128)S(1)}, u32[]{:S(2)}, u32[]{:S(2)}) %collective-permute-start.8) | collective-permute-done | bytes 5152 | tf_op jit(solution)/shard_map/ppermute | solution.py:21
  100.2 0.6 collective-permute-start.13
  100.8 0.1 collective-permute-done.9
  100.9 0.9 collective-permute-start.14
  101.7 0.0 collective-permute-done.10
  101.7 2.9 %collective-permute-start.15 = (f32[8,160]{1,0:T(8,128)}, f32[8,160]{1,0:T(8,128)S(1)}, u32[]{:S(2)}, u32[]{:S(2)}) collective-permute-start(f32[8,160]{1,0:T(8,128)} %get-tuple-element.21), channel_id=1, source_target_pairs={{0,28},{1,29},{2,30},{3,31},{4,0},{5,1},{6,2},{7,3},{8,4},{9,5},{1... | collective-permute-start | bytes 15368 | tf_op jit(solution)/shard_map/ppermute | solution.py:21
  104.7 0.7 add_add_fusion
  105.4 0.0 collective-permute-done.11
  105.4 0.0 collective-permute-done.12
  105.4 0.0 collective-permute-done.13
  105.4 0.0 collective-permute-done.14
  105.4 0.8 collective-permute-done.15
  106.2 0.6 slice_add_fusion
Async XLA Ops:
  0.6 27.5 %copy-start = (s32[1,160]{1,0:T(1,128)S(1)}, s32[1,160]{1,0:T(1,128)}, u32[]{:S(2)}) copy-start(s32[1,160]{1,0:T(1,128)} %param.9) | copy-start | bytes 1924
  2.2 20.6 %collective-permute-start.7 = (f32[80,640]{1,0:T(8,128)S(1)}, f32[80,640]{1,0:T(8,128)S(1)}, u32[]{:S(2)}, u32[]{:S(2)}) collective-permute-start(f32[80,640]{1,0:T(8,128)S(1)} %get-tuple-element.22), channel_id=1, source_target_pairs={{0,4},{1,5},{2,6},{3,7},{4,8},{5,9},{6,10},{7,11},{8,12},{9,13},{1... | collective-permute-start | bytes 614408 | tf_op jit(solution)/shard_map/ppermute | solution.py:21
  5.3 17.5 %collective-permute-start.5 = (f32[80,640]{1,0:T(8,128)S(1)}, f32[80,640]{1,0:T(8,128)S(1)}, u32[]{:S(2)}, u32[]{:S(2)}) collective-permute-start(f32[80,640]{1,0:T(8,128)S(1)} %get-tuple-element.23), channel_id=1, source_target_pairs={{0,2},{1,3},{2,4},{3,5},{4,6},{5,7},{6,8},{7,9},{8,10},{9,11},{10,... | collective-permute-start | bytes 614408 | tf_op jit(solution)/shard_map/ppermute | solution.py:21
  6.7 21.4 %collective-permute-start.4 = (f32[80,640]{1,0:T(8,128)S(1)}, f32[80,640]{1,0:T(8,128)S(1)}, u32[]{:S(2)}, u32[]{:S(2)}) collective-permute-start(f32[80,640]{1,0:T(8,128)S(1)} %get-tuple-element.24), channel_id=1, source_target_pairs={{0,1},{1,2},{2,3},{3,4},{4,5},{5,6},{6,7},{7,8},{8,9},{9,10},{10,1... | collective-permute-start | bytes 614408 | tf_op jit(solution)/shard_map/ppermute | solution.py:21
  6.8 37.2 %collective-permute-start.3 = (f32[80,640]{1,0:T(8,128)S(1)}, f32[80,640]{1,0:T(8,128)S(1)}, u32[]{:S(2)}, u32[]{:S(2)}) collective-permute-start(f32[80,640]{1,0:T(8,128)S(1)} %get-tuple-element.25), channel_id=1, source_target_pairs={{0,28},{1,29},{2,30},{3,31},{4,0},{5,1},{6,2},{7,3},{8,4},{9,5},{1... | collective-permute-start | bytes 614408 | tf_op jit(solution)/shard_map/ppermute | solution.py:21
  10.0 34.0 %collective-permute-start.2 = (f32[80,640]{1,0:T(8,128)S(1)}, f32[80,640]{1,0:T(8,128)S(1)}, u32[]{:S(2)}, u32[]{:S(2)}) collective-permute-start(f32[80,640]{1,0:T(8,128)S(1)} %get-tuple-element.26), channel_id=1, source_target_pairs={{0,29},{1,30},{2,31},{3,0},{4,1},{5,2},{6,3},{7,4},{8,5},{9,6},{10... | collective-permute-start | bytes 614408 | tf_op jit(solution)/shard_map/ppermute | solution.py:21
  22.8 20.6 %copy-start.1 = (f32[80,640]{1,0:T(8,128)}, f32[80,640]{1,0:T(8,128)S(1)}, u32[]{:S(2)}) copy-start(f32[80,640]{1,0:T(8,128)S(1)} %collective-permute-done.7.refs_7_) | copy-start | bytes 614404
  22.8 21.2 %collective-permute-start.1 = (f32[80,640]{1,0:T(8,128)S(1)}, f32[80,640]{1,0:T(8,128)S(1)}, u32[]{:S(2)}, u32[]{:S(2)}) collective-permute-start(f32[80,640]{1,0:T(8,128)S(1)} %get-tuple-element.27), channel_id=1, source_target_pairs={{0,30},{1,31},{2,0},{3,1},{4,2},{5,3},{6,4},{7,5},{8,6},{9,7},{10,... | collective-permute-start | bytes 614408 | tf_op jit(solution)/shard_map/ppermute | solution.py:21
  22.8 20.5 %copy-start.2 = (f32[80,640]{1,0:T(8,128)}, f32[80,640]{1,0:T(8,128)S(1)}, u32[]{:S(2)}) copy-start(f32[80,640]{1,0:T(8,128)S(1)} %collective-permute-done.5.refs_5_) | copy-start | bytes 614404
  22.8 21.2 %collective-permute-start = (f32[80,640]{1,0:T(8,128)S(1)}, f32[80,640]{1,0:T(8,128)S(1)}, u32[]{:S(2)}, u32[]{:S(2)}) collective-permute-start(f32[80,640]{1,0:T(8,128)S(1)} %get-tuple-element.28), channel_id=1, source_target_pairs={{0,31},{1,0},{2,1},{3,2},{4,3},{5,4},{6,5},{7,6},{8,7},{9,8},{10,9... | collective-permute-start | bytes 614408 | tf_op jit(solution)/shard_map/ppermute | solution.py:21
  28.1 15.2 %copy-start.3 = (f32[80,640]{1,0:T(8,128)}, f32[80,640]{1,0:T(8,128)S(1)}, u32[]{:S(2)}) copy-start(f32[80,640]{1,0:T(8,128)S(1)} %collective-permute-done.4.refs_4_) | copy-start | bytes 614404
  28.1 15.9 %collective-permute-start.6 = (f32[80,640]{1,0:T(8,128)S(1)}, f32[80,640]{1,0:T(8,128)S(1)}, u32[]{:S(2)}, u32[]{:S(2)}) collective-permute-start(f32[80,640]{1,0:T(8,128)S(1)} %get-tuple-element.29), channel_id=1, source_target_pairs={{0,3},{1,4},{2,5},{3,6},{4,7},{5,8},{6,9},{7,10},{8,11},{9,12},{10... | collective-permute-start | bytes 614408 | tf_op jit(solution)/shard_map/ppermute | solution.py:21
  44.0 0.7 copy-start.4
  44.0 0.8 copy-start.5
  44.0 0.8 copy-start.6
  44.0 0.8 copy-start.7
  44.8 0.7 copy-start.8
  93.3 6.9 %collective-permute-start.8 = (f32[8,160]{1,0:T(8,128)}, f32[8,160]{1,0:T(8,128)S(1)}, u32[]{:S(2)}, u32[]{:S(2)}) collective-permute-start(f32[8,160]{1,0:T(8,128)} %get-tuple-element.14), channel_id=1, source_target_pairs={{0,1},{1,2},{2,3},{3,4},{4,5},{5,6},{6,7},{7,8},{8,9},{9,10},{10,1... | collective-permute-start | bytes 15368 | tf_op jit(solution)/shard_map/ppermute | solution.py:21
  93.4 7.5 %collective-permute-start.9 = (f32[8,160]{1,0:T(8,128)}, f32[8,160]{1,0:T(8,128)S(1)}, u32[]{:S(2)}, u32[]{:S(2)}) collective-permute-start(f32[8,160]{1,0:T(8,128)} %get-tuple-element.15), channel_id=1, source_target_pairs={{0,2},{1,3},{2,4},{3,5},{4,6},{5,7},{6,8},{7,9},{8,10},{9,11},{10,... | collective-permute-start | bytes 15368 | tf_op jit(solution)/shard_map/ppermute | solution.py:21
  93.4 8.3 %collective-permute-start.10 = (f32[8,160]{1,0:T(8,128)}, f32[8,160]{1,0:T(8,128)S(1)}, u32[]{:S(2)}, u32[]{:S(2)}) collective-permute-start(f32[8,160]{1,0:T(8,128)} %get-tuple-element.16), channel_id=1, source_target_pairs={{0,3},{1,4},{2,5},{3,6},{4,7},{5,8},{6,9},{7,10},{8,11},{9,12},{10... | collective-permute-start | bytes 15368 | tf_op jit(solution)/shard_map/ppermute | solution.py:21
  93.8 11.5 %collective-permute-start.11 = (f32[8,160]{1,0:T(8,128)}, f32[8,160]{1,0:T(8,128)S(1)}, u32[]{:S(2)}, u32[]{:S(2)}) collective-permute-start(f32[8,160]{1,0:T(8,128)} %get-tuple-element.17), channel_id=1, source_target_pairs={{0,4},{1,5},{2,6},{3,7},{4,8},{5,9},{6,10},{7,11},{8,12},{9,13},{1... | collective-permute-start | bytes 15368 | tf_op jit(solution)/shard_map/ppermute | solution.py:21
  96.1 9.3 %collective-permute-start.12 = (f32[8,160]{1,0:T(8,128)}, f32[8,160]{1,0:T(8,128)S(1)}, u32[]{:S(2)}, u32[]{:S(2)}) collective-permute-start(f32[8,160]{1,0:T(8,128)} %get-tuple-element.18), channel_id=1, source_target_pairs={{0,31},{1,0},{2,1},{3,2},{4,3},{5,4},{6,5},{7,6},{8,7},{9,8},{10,9... | collective-permute-start | bytes 15368 | tf_op jit(solution)/shard_map/ppermute | solution.py:21
  100.2 5.2 %collective-permute-start.13 = (f32[8,160]{1,0:T(8,128)}, f32[8,160]{1,0:T(8,128)S(1)}, u32[]{:S(2)}, u32[]{:S(2)}) collective-permute-start(f32[8,160]{1,0:T(8,128)} %get-tuple-element.19), channel_id=1, source_target_pairs={{0,30},{1,31},{2,0},{3,1},{4,2},{5,3},{6,4},{7,5},{8,6},{9,7},{10,... | collective-permute-start | bytes 15368 | tf_op jit(solution)/shard_map/ppermute | solution.py:21
  100.9 4.5 %collective-permute-start.14 = (f32[8,160]{1,0:T(8,128)}, f32[8,160]{1,0:T(8,128)S(1)}, u32[]{:S(2)}, u32[]{:S(2)}) collective-permute-start(f32[8,160]{1,0:T(8,128)} %get-tuple-element.20), channel_id=1, source_target_pairs={{0,29},{1,30},{2,31},{3,0},{4,1},{5,2},{6,3},{7,4},{8,5},{9,6},{10... | collective-permute-start | bytes 15368 | tf_op jit(solution)/shard_map/ppermute | solution.py:21
  101.7 4.5 %collective-permute-start.15 = (f32[8,160]{1,0:T(8,128)}, f32[8,160]{1,0:T(8,128)S(1)}, u32[]{:S(2)}, u32[]{:S(2)}) collective-permute-start(f32[8,160]{1,0:T(8,128)} %get-tuple-element.21), channel_id=1, source_target_pairs={{0,28},{1,29},{2,30},{3,31},{4,0},{5,1},{6,2},{7,3},{8,4},{9,5},{1... | collective-permute-start | bytes 15368 | tf_op jit(solution)/shard_map/ppermute | solution.py:21

commit v2 on v1

--- a/solution.py
+++ b/solution.py
@@ -53,10 +53,9 @@
 ):
     block_count = 2 * NB
     pieces = refs[:block_count]
-    density_out, own_out = refs[block_count : block_count + 2]
-    halo_outs = refs[block_count + 2 : 2 * block_count + 2]
-    (x, high_a, low_a, high_b, low_b, halo, density, deriv_held, row_part, deriv_sems, out_sem) = refs[
-        2 * block_count + 2 :
+    density_out, own_out, near_up, near_down, far_up, far_down = refs[block_count : block_count + 6]
+    (x, high_a, low_a, high_b, low_b, diag_row_a, diag_row_b, diag_col_a, diag_col_b, halo, density, deriv_held, row_part, deriv_sems, out_sem) = refs[
+        block_count + 6 :
     ]
     rows, order = core.shape
     atoms = rows // ORB
@@ -74,12 +73,19 @@
         halo[block * slot_rows : (block + 1) * slot_rows, :] = pieces[block][...]
     live_row = (request_row[...] >= 0).astype(jnp.float32)
     live_col = (request_col[...] >= 0).astype(jnp.float32)
-    eye = (
-        lax.broadcasted_iota(jnp.int32, (SUB, SUB), 0) == lax.broadcasted_iota(jnp.int32, (SUB, SUB), 1)
-    ).astype(jnp.float32)
+    eye = lax.broadcasted_iota(jnp.int32, (SUB, SUB), 0) == lax.broadcasted_iota(jnp.int32, (SUB, SUB), 1)
 
     def put(value, row, col):
         x[row : row + SUB, col : col + SUB] = value
+        if row == col:
+            line = jnp.where(eye, value, 0.0)
+            diag_row_a[:, col : col + SUB] = jnp.broadcast_to(
+                jnp.sum(line, axis=0, keepdims=True), (8, SUB)
+            )
+            diag_col_a[row : row + SUB, :] = jnp.broadcast_to(
+                jnp.sum(line, axis=1, keepdims=True), (SUB, SUB)
+            )
+            value = value - line
         high, low = halves(value)
         high_a[row : row + SUB, col : col + SUB] = high
         low_a[row : row + SUB, col : col + SUB] = low
@@ -95,7 +101,7 @@
                 core[row : row + SUB, col : col + SUB] + core[col : col + SUB, row : row + SUB].T
             )
             if row == col:
-                value = value - top * eye
+                value = value - jnp.where(eye, top, 0.0)
             put(-scale * value, row, col)
     for row in range(0, rows, SUB):
         for col in range(rows, order, SUB):
@@ -107,48 +113,80 @@
                 halo[row : row + SUB, col : col + SUB] + halo[col : col + SUB, row : row + SUB].T
             )
             if row == col:
-                value = value - top * eye
+                value = value - jnp.where(eye, top, 0.0)
             value = value * live_col[row : row + SUB, :] * live_row[:, col : col + SUB]
             put(-scale * value, row + rows, col + rows)
 
-    def product(high, low, upto, cols):
-        right_high, right_low = high[:, cols], low[:, cols]
-        left_high, left_low = high[0:upto, :], low[0:upto, :]
-        return dot(left_high, right_high) + (dot(left_high, right_low) + dot(left_low, right_high))
-
-    def factors(number):
+    def stepped(number, now, rows_at, cols_at):
+        high, low, diag_row, diag_col = now
         taken = (branches[number] == 1).astype(jnp.float32)
-        return 2.0 * taken, 1.0 - 2.0 * taken
-
-    def squaring(number, high, low, next_high, next_low):
-        keep, add = factors(number)
+        keep, add = 2.0 * taken, 1.0 - 2.0 * taken
+        left_high, left_low = high[rows_at, :], low[rows_at, :]
+        right_high, right_low = high[:, cols_at], low[:, cols_at]
+        if rows_at == cols_at:
+            cross = dot(left_high, right_low)
+            off = dot(left_high, right_high) + (cross + cross.T)
+        else:
+            off = dot(
+                jnp.concatenate([left_high, left_high, left_low], axis=1),
+                jnp.concatenate([right_high, right_low, right_high], axis=0),
+            )
+        old = x[rows_at, cols_at]
+        factor_col = keep + add * diag_col[rows_at, :]
+        factor = jnp.concatenate([factor_col, factor_col], axis=1) + add * diag_row[0:1, cols_at]
+        value = old * factor + add * off
+        if rows_at.start == cols_at.start:
+            on = lax.broadcasted_iota(jnp.int32, value.shape, 0) == lax.broadcasted_iota(
+                jnp.int32, value.shape, 1
+            )
+            value = value - jnp.where(on, add * (old * old), 0.0)
+        return value
+
+    def squaring(number, now, later):
+        next_high, next_low, next_row, next_col = later
         for start in range(0, order, PANEL):
-            end = start + PANEL
-            cols = slice(start, end)
-            value = keep * x[0:end, cols] + add * product(high, low, end, cols)
-            x[0:end, cols] = value
-            new_high, new_low = halves(value)
-            next_high[0:end, cols] = new_high
-            next_low[0:end, cols] = new_low
-            if start > 0:
-                next_high[cols, 0:start] = new_high[0:start].T
-                next_low[cols, 0:start] = new_low[0:start].T
+            cols = slice(start, start + PANEL)
+            for at in range(0, start + PANEL, PANEL):
+                lines = slice(at, at + PANEL)
+                value = stepped(number, now, lines, cols)
+                x[lines, cols] = value
+                if at == start:
+                    on = lax.broadcasted_iota(jnp.int32, value.shape, 0) == lax.broadcasted_iota(
+                        jnp.int32, value.shape, 1
+                    )
+                    line = jnp.where(on, value, 0.0)
+                    next_row[:, cols] = jnp.broadcast_to(
+                        jnp.sum(line, axis=0, keepdims=True), (8, PANEL)
+                    )
+                    next_col[cols, :] = jnp.broadcast_to(
+                        jnp.sum(line, axis=1, keepdims=True), (PANEL, SUB)
+                    )
+                    value = value - line
+                new_high, new_low = halves(value)
+                next_high[lines, cols] = new_high
+                next_low[lines, cols] = new_low
+                if at < start:
+                    next_high[cols, lines] = new_high.T
+                    next_low[cols, lines] = new_low.T
+
+    state_a = (high_a, low_a, diag_row_a, diag_col_a)
+    state_b = (high_b, low_b, diag_row_b, diag_col_b)
 
     def two(pair, carry):
-        squaring(2 * pair, high_a, low_a, high_b, low_b)
-        squaring(2 * pair + 1, high_b, low_b, high_a, low_a)
+        squaring(2 * pair, state_a, state_b)
+        squaring(2 * pair + 1, state_b, state_a)
         return carry
 
     lax.fori_loop(0, (ITERS - 1) // 2, two, 0)
-    keep, add = factors(ITERS - 1)
     for start in range(0, order, PANEL):
-        upto = min(start + PANEL, rows)
         cols = slice(start, start + PANEL)
-        value = keep * x[0:upto, cols] + add * product(high_a, low_a, upto, cols)
-        density[0:upto, cols] = value
-        if 0 < start < rows:
-            end = min(start + PANEL, rows)
-            density[start:end, 0:start] = value[0:start, 0 : end - start].T
+        for at in range(0, min(start + PANEL, rows), PANEL):
+            lines = slice(at, min(at + PANEL, rows))
+            value = stepped(ITERS - 1, state_a, lines, cols)
+            density[lines, cols] = value
+            if at < start < rows:
+                end = min(start + PANEL, rows)
+                density[start:end, lines] = value[:, 0 : end - start].T
 
     out_copy = pltpu.make_async_copy(density, density_out, out_sem)
     out_copy.start()
@@ -184,8 +222,13 @@
         [jnp.where(lane_block == block, halo_columns, 0.0) for block in range(block_count)], axis=0
     )
     terms = dot_one_hot(spread, asked_hot)
-    for block in range(block_count):
-        halo_outs[block][...] = terms[8 * block : 8 * block + 8, :]
+    places = {
+        block_offset(block): terms[8 * block : 8 * block + 8, :] for block in range(block_count)
+    }
+    near_up[...] = jnp.concatenate([places[1], places[4], places[-2]], axis=0)
+    near_down[...] = jnp.concatenate([places[-1], places[-4], places[2]], axis=0)
+    far_up[...] = places[3]
+    far_down[...] = places[-3]
     out_copy.wait()
 
 
@@ -197,18 +240,23 @@
     smem = pl.BlockSpec(memory_space=pltpu.SMEM)
     anywhere = pl.BlockSpec(memory_space=pl.ANY)
     square = (order, order)
-    small = jax.ShapeDtypeStruct((8, atoms), jnp.float32)
+    one = jax.ShapeDtypeStruct((8, atoms), jnp.float32)
+    three = jax.ShapeDtypeStruct((24, atoms), jnp.float32)
     return pl.pallas_call(
         kernel,
-        out_shape=[jax.ShapeDtypeStruct((rows, order), jnp.float32)] + [small] * (block_count + 1),
+        out_shape=[jax.ShapeDtypeStruct((rows, order), jnp.float32), one, three, three, one, one],
         in_specs=[smem, smem, vmem, vmem, vmem, anywhere] + [vmem] * block_count,
-        out_specs=[anywhere] + [vmem] * (block_count + 1),
+        out_specs=[anywhere] + [vmem] * 5,
         scratch_shapes=[
             pltpu.VMEM(square, jnp.float32),
             pltpu.VMEM(square, jnp.bfloat16),
             pltpu.VMEM(square, jnp.bfloat16),
             pltpu.VMEM(square, jnp.bfloat16),
             pltpu.VMEM(square, jnp.bfloat16),
+            pltpu.VMEM((8, order), jnp.float32),
+            pltpu.VMEM((8, order), jnp.float32),
+            pltpu.VMEM((order, SUB), jnp.float32),
+            pltpu.VMEM((order, SUB), jnp.float32),
             pltpu.VMEM((order - rows, order - rows), jnp.float32),
             pltpu.VMEM((rows, order), jnp.float32),
             pltpu.VMEM((3, rows, order), jnp.float32),
@@ -226,23 +274,30 @@
 def per_device(ham_core, halo_rows, halo_request, deriv, e_low, e_high, branches):
     row_count, order_all = ham_core.shape
     block_count = 2 * NB
-    pieces = [
-        passed_along(halo_rows[0, block, :, row_count:], "dom", -block_offset(block))
-        for block in range(block_count)
-    ]
+    halo = halo_rows[0, :, :, row_count:]
+    flat_deriv = deriv.reshape(3, row_count, order_all)
+    early = (1, 2, 3, 5, 6)
+    late = (0, 4, 7)
+    pieces = {block: passed_along(halo[block], "dom", -block_offset(block)) for block in early}
+    waiting, flat_deriv = lax.optimization_barrier(([halo[block] for block in late], flat_deriv))
+    for block, piece in zip(late, waiting):
+        pieces[block] = passed_along(piece, "dom", -block_offset(block))
     request = jnp.repeat(halo_request[0], ORB)
-    outs = density_and_terms(
+    density, forces, near_up, near_down, far_up, far_down = density_and_terms(
         jnp.concatenate([e_high, e_low]),
         branches,
         ham_core,
         request[None, :],
         request[:, None],
-        deriv.reshape(3, row_count, order_all),
-        pieces,
+        flat_deriv,
+        [pieces[block] for block in range(block_count)],
     )
-    density, forces = outs[:2]
-    for block in range(block_count):
-        forces = forces + passed_along(outs[2 + block], "dom", block_offset(block))
+    from_below = passed_along(near_up, "dom", 1)
+    from_above = passed_along(near_down, "dom", -1)
+    far_up = far_up + (from_below[8:16] + from_above[16:24])
+    far_down = far_down + (from_above[8:16] + from_below[16:24])
+    forces = forces + (from_below[:8] + from_above[:8])
+    forces = forces + (passed_along(far_up, "dom", 3) + passed_along(far_down, "dom", -3))
     return (density, forces[:3])
 
 

time: 107 us -> 99.3 us (0.928)
  Pallas kernels: 47.8 us -> 43.5 us
  waiting for transfers between devices: 13.8 us -> 10.2 us
    pallas_call x1, Pallas kernels: 47.8 us -> 43.5 us  [density_and_terms(): pl.pallas_call(kernel, out_shape=[jax.ShapeDtypeStruct((rows, order), jnp...]
    ppermute x16 -> x12, waiting for transfers between devices: 13.8 us -> 10.2 us  [passed_along(): return lax.ppermute(value, axis, pairs)]
    ppermute x16 -> x12, starting transfers between devices: 24.3 us -> 23.6 us  [passed_along(): return lax.ppermute(value, axis, pairs)]
  transfers between devices with their start and end apart: 16 -> 12, of which waited for: 4 -> 3; matrix products, arithmetic and copies ran while one was open for 14% -> 15% of each run, Pallas kernels for 0% -> 0%
where the time goes in v2:
time: 99.3 us; the launch traced here: 98.8 us
  Pallas kernels  43.5 us (44%)
  starting transfers between devices  23.6 us (24%)
  local copies, waits for them, and re-layouts  16.8 us (17%)
  waiting for transfers between devices  10.2 us (10%)
  other arithmetic  2.61 us (3%)
  between operations  2.08 us (2%)
    pallas_call x1, Pallas kernels, density_and_terms(): pl.pallas_call(kernel, out_shape=[jax.ShapeDtypeStruct((rows, order), jnp...  43.5 us
    ppermute x12, starting transfers between devices, passed_along(): return lax.ppermute(value, axis, pairs)  23.6 us
    reshape x1, local copies, waits for them, and re-layouts, per_device(): flat_deriv = deriv.reshape(3, row_count, order_all)  12.3 us
    ppermute x12, waiting for transfers between devices, passed_along(): return lax.ppermute(value, axis, pairs)  10.2 us
  transfers between devices with their start and end apart: 12, of which 3 were waited for; matrix products, arithmetic and copies ran while one was open for 15% of the time, Pallas kernels for 0%

profile of v2, /device:TPU:0, one launch (start us, length us, event | category | flops | bytes accessed | tf_op | source)
XLA Modules:
  0.0 98.8 jit_solution(15342993999530843337)
XLA Ops:
  0.6 1.6 %slice_bitcast_fusion = (f32[80,640]{1,0:T(8,128)S(1)}, f32[80,640]{1,0:T(8,128)S(1)}, f32[80,640]{1,0:T(8,128)S(1)}, f32[80,640]{1,0:T(8,128)S(1)}, f32[80,640]...) fusion(f32[1,8,80,1280]{3,2,1,0:T(8,128)} %param.8), kind=kLoop, calls=%fused_computation | loop fusion | bytes 3276800 | tf_op jit(solution)/shard_map/squeeze | solution.py:281
  2.2 2.4 %collective-permute-start.6 = (f32[80,640]{1,0:T(8,128)S(1)}, f32[80,640]{1,0:T(8,128)S(1)}, u32[]{:S(2)}, u32[]{:S(2)}) collective-permute-start(f32[80,640]{1,0:T(8,128)S(1)} %get-tuple-element.22), channel_id=1, source_target_pairs={{0,3},{1,4},{2,5},{3,6},{4,7},{5,8},{6,9},{7,10},{8,11},{9,12},{10... | collective-permute-start | bytes 614408 | tf_op jit(solution)/shard_map/ppermute | solution.py:21
  4.7 4.6 %collective-permute-start.3 = (f32[80,640]{1,0:T(8,128)S(1)}, f32[80,640]{1,0:T(8,128)S(1)}, u32[]{:S(2)}, u32[]{:S(2)}) collective-permute-start(f32[80,640]{1,0:T(8,128)S(1)} %get-tuple-element.23), channel_id=1, source_target_pairs={{0,28},{1,29},{2,30},{3,31},{4,0},{5,1},{6,2},{7,3},{8,4},{9,5},{1... | collective-permute-start | bytes 614408 | tf_op jit(solution)/shard_map/ppermute | solution.py:21
  9.2 0.5 collective-permute-start.2
  9.8 2.3 %collective-permute-start.1 = (f32[80,640]{1,0:T(8,128)S(1)}, f32[80,640]{1,0:T(8,128)S(1)}, u32[]{:S(2)}, u32[]{:S(2)}) collective-permute-start(f32[80,640]{1,0:T(8,128)S(1)} %get-tuple-element.25), channel_id=1, source_target_pairs={{0,30},{1,31},{2,0},{3,1},{4,2},{5,3},{6,4},{7,5},{8,6},{9,7},{10,... | collective-permute-start | bytes 614408 | tf_op jit(solution)/shard_map/ppermute | solution.py:21
  12.1 0.0 copy-start
  12.1 0.0 collective-permute-start.5
  12.1 12.3 %reshape.23.deriv = f32[3,640,1280]{2,1,0:T(8,128)} reshape(f32[3,160,4,1280]{3,2,1,0:T(4,128)} %param.10) | data formatting | bytes 19660800 | tf_op jit(solution)/shard_map/reshape | solution.py:278
  24.4 0.0 collective-permute-done.6.refs_6_
  24.4 0.0 copy-start.1
  24.4 3.9 %collective-permute-start = (f32[80,640]{1,0:T(8,128)S(1)}, f32[80,640]{1,0:T(8,128)S(1)}, u32[]{:S(2)}, u32[]{:S(2)}) collective-permute-start(f32[80,640]{1,0:T(8,128)S(1)} %get-tuple-element.13), channel_id=1, source_target_pairs={{0,31},{1,0},{2,1},{3,2},{4,3},{5,4},{6,5},{7,6},{8,7},{9,8},{10,9... | collective-permute-start | bytes 614408 | tf_op jit(solution)/shard_map/ppermute | solution.py:21
  28.3 0.0 collective-permute-done.3.refs_3_
  28.3 0.0 copy-start.2
  28.3 0.0 collective-permute-start.4
  28.3 0.0 collective-permute-done.2.refs_2_
  28.3 0.0 copy-start.3
  28.3 0.1 collective-permute-start.7
  28.4 0.0 copy-done
  28.4 0.1 broadcast_in_dim.3
  28.5 0.7 broadcast_in_dim_reshape.6.request_row
  29.1 0.9 broadcast_in_dim_reshape.8.request_col
  31.3 0.6 pad_maximum_fusion.ends
  31.9 0.0 collective-permute-done.1.refs_1_
  31.9 0.0 copy-start.4
  31.9 0.0 collective-permute-done.5.refs_5_
  31.9 0.0 copy-start.5
  31.9 0.0 collective-permute-done.refs_0_
  31.9 0.0 copy-start.6
  31.9 7.1 %collective-permute-done.4.refs_4_ = f32[80,640]{1,0:T(8,128)S(1)} collective-permute-done((f32[80,640]{1,0:T(8,128)S(1)}, f32[80,640]{1,0:T(8,128)S(1)}, u32[]{:S(2)}, u32[]{:S(2)}) %collective-permute-start.4) | collective-permute-done | bytes 204832 | tf_op jit(solution)/shard_map/ppermute | solution.py:21
  39.0 0.0 copy-start.7
  39.0 0.0 collective-permute-done.7.refs_7_
  39.0 0.0 copy-done.1
  39.0 0.0 copy-done.2
  39.0 0.0 copy-done.3
  39.0 0.0 copy-done.4
  39.0 0.0 copy-done.5
  39.0 0.0 copy-done.6
  39.1 0.6 copy-done.7
  39.7 0.0 copy-start.8
  39.7 0.7 copy-done.8
  40.4 43.5 %shard_map.86 = (f32[640,1280]{1,0:T(8,128)}, f32[8,160]{1,0:T(8,128)}, f32[24,160]{1,0:T(8,128)}, f32[24,160]{1,0:T(8,128)}, f32[8,160]{1,0:T(8,128)}, /*index=5*/f32[8,160]{1,0:T(8,128)}) custom-call(f32[2]{0:T(128)} %pad_maximum_fusion.ends, s32[5]{0:T(128)} %branches.1, f32[640,1280]{1,0:T(8,128)} %core.1, s32[1,640]{1,0:T(1,128)} %broadcast_in_dim_reshape.6.request_row, ...), custom_call_target="tpu_custom_call" | custom-call | flops 37748736000 | bytes 24000000 | tf_op jit(solution)/shard_map/pallas_call | solution.py:245
  83.8 0.1 collective-permute-start.8
  83.9 5.3 %collective-permute-start.9 = (f32[24,160]{1,0:T(8,128)}, f32[24,160]{1,0:T(8,128)S(1)}, u32[]{:S(2)}, u32[]{:S(2)}) collective-permute-start(f32[24,160]{1,0:T(8,128)} %get-tuple-element.19), channel_id=1, source_target_pairs={{0,31},{1,0},{2,1},{3,2},{4,3},{5,4},{6,5},{7,6},{8,7},{9,8},{10,9... | collective-permute-start | bytes 46088 | tf_op jit(solution)/shard_map/ppermute | solution.py:21
  89.2 1.7 %collective-permute-done.8 = f32[24,160]{1,0:T(8,128)S(1)} collective-permute-done((f32[24,160]{1,0:T(8,128)}, f32[24,160]{1,0:T(8,128)S(1)}, u32[]{:S(2)}, u32[]{:S(2)}) %collective-permute-start.8) | collective-permute-done | bytes 15392 | tf_op jit(solution)/shard_map/ppermute | solution.py:21
  91.0 0.0 collective-permute-done.9
  91.0 0.7 fusion.1
  91.7 0.0 collective-permute-start.10
  91.7 4.4 %collective-permute-start.11 = (f32[8,160]{1,0:T(8,128)S(1)}, f32[8,160]{1,0:T(8,128)S(1)}, u32[]{:S(2)}, u32[]{:S(2)}) collective-permute-start(f32[8,160]{1,0:T(8,128)S(1)} %get-tuple-element.31), channel_id=1, source_target_pairs={{0,29},{1,30},{2,31},{3,0},{4,1},{5,2},{6,3},{7,4},{8,5},{9,6},{10... | collective-permute-start | bytes 15368 | tf_op jit(solution)/shard_map/ppermute | solution.py:21
  96.1 1.3 %collective-permute-done.10 = f32[8,160]{1,0:T(8,128)S(1)} collective-permute-done((f32[8,160]{1,0:T(8,128)S(1)}, f32[8,160]{1,0:T(8,128)S(1)}, u32[]{:S(2)}, u32[]{:S(2)}) %collective-permute-start.10) | collective-permute-done | bytes 5152 | tf_op jit(solution)/shard_map/ppermute | solution.py:21
  97.5 0.0 collective-permute-done.11
  97.5 1.3 %fusion.2 = f32[3,160]{1,0:T(4,128)} fusion(f32[8,160]{1,0:T(8,128)S(1)} %collective-permute-done.11, f32[8,160]{1,0:T(8,128)S(1)} %collective-permute-done.10, f32[8,160]{1,0:T(8,128)} %get-tuple-element.17, f32[8,160]{1,0:T(8,128)S(1)} %get-tuple-element.33, f32[8,160]{1,0:T(8,128)S(1)} %get-tuple-element.32), kind=kLoop, calls=%fused_computation.13 | loop fusion | flops 1920 | bytes 11520 | tf_op jit(solution)/shard_map/add | solution.py:300
Async XLA Ops:
  2.2 22.1 %collective-permute-start.6 = (f32[80,640]{1,0:T(8,128)S(1)}, f32[80,640]{1,0:T(8,128)S(1)}, u32[]{:S(2)}, u32[]{:S(2)}) collective-permute-start(f32[80,640]{1,0:T(8,128)S(1)} %get-tuple-element.22), channel_id=1, source_target_pairs={{0,3},{1,4},{2,5},{3,6},{4,7},{5,8},{6,9},{7,10},{8,11},{9,12},{10... | collective-permute-start | bytes 614408 | tf_op jit(solution)/shard_map/ppermute | solution.py:21
  4.7 23.6 %collective-permute-start.3 = (f32[80,640]{1,0:T(8,128)S(1)}, f32[80,640]{1,0:T(8,128)S(1)}, u32[]{:S(2)}, u32[]{:S(2)}) collective-permute-start(f32[80,640]{1,0:T(8,128)S(1)} %get-tuple-element.23), channel_id=1, source_target_pairs={{0,28},{1,29},{2,30},{3,31},{4,0},{5,1},{6,2},{7,3},{8,4},{9,5},{1... | collective-permute-start | bytes 614408 | tf_op jit(solution)/shard_map/ppermute | solution.py:21
  9.2 19.1 %collective-permute-start.2 = (f32[80,640]{1,0:T(8,128)S(1)}, f32[80,640]{1,0:T(8,128)S(1)}, u32[]{:S(2)}, u32[]{:S(2)}) collective-permute-start(f32[80,640]{1,0:T(8,128)S(1)} %get-tuple-element.24), channel_id=1, source_target_pairs={{0,29},{1,30},{2,31},{3,0},{4,1},{5,2},{6,3},{7,4},{8,5},{9,6},{10... | collective-permute-start | bytes 614408 | tf_op jit(solution)/shard_map/ppermute | solution.py:21
  9.8 22.1 %collective-permute-start.1 = (f32[80,640]{1,0:T(8,128)S(1)}, f32[80,640]{1,0:T(8,128)S(1)}, u32[]{:S(2)}, u32[]{:S(2)}) collective-permute-start(f32[80,640]{1,0:T(8,128)S(1)} %get-tuple-element.25), channel_id=1, source_target_pairs={{0,30},{1,31},{2,0},{3,1},{4,2},{5,3},{6,4},{7,5},{8,6},{9,7},{10,... | collective-permute-start | bytes 614408 | tf_op jit(solution)/shard_map/ppermute | solution.py:21
  12.1 16.3 %copy-start = (s32[1,160]{1,0:T(1,128)S(1)}, s32[1,160]{1,0:T(1,128)}, u32[]{:S(2)}) copy-start(s32[1,160]{1,0:T(1,128)} %param.9) | copy-start | bytes 1924
  12.1 19.8 %collective-permute-start.5 = (f32[80,640]{1,0:T(8,128)S(1)}, f32[80,640]{1,0:T(8,128)S(1)}, u32[]{:S(2)}, u32[]{:S(2)}) collective-permute-start(f32[80,640]{1,0:T(8,128)S(1)} %get-tuple-element.29), channel_id=1, source_target_pairs={{0,2},{1,3},{2,4},{3,5},{4,6},{5,7},{6,8},{7,9},{8,10},{9,11},{10,... | collective-permute-start | bytes 614408 | tf_op jit(solution)/shard_map/ppermute | solution.py:21
  24.4 14.6 %copy-start.1 = (f32[80,640]{1,0:T(8,128)}, f32[80,640]{1,0:T(8,128)S(1)}, u32[]{:S(2)}) copy-start(f32[80,640]{1,0:T(8,128)S(1)} %collective-permute-done.6.refs_6_) | copy-start | bytes 614404
  24.4 7.5 %collective-permute-start = (f32[80,640]{1,0:T(8,128)S(1)}, f32[80,640]{1,0:T(8,128)S(1)}, u32[]{:S(2)}, u32[]{:S(2)}) collective-permute-start(f32[80,640]{1,0:T(8,128)S(1)} %get-tuple-element.13), channel_id=1, source_target_pairs={{0,31},{1,0},{2,1},{3,2},{4,3},{5,4},{6,5},{7,6},{8,7},{9,8},{10,9... | collective-permute-start | bytes 614408 | tf_op jit(solution)/shard_map/ppermute | solution.py:21
  28.3 10.7 %copy-start.2 = (f32[80,640]{1,0:T(8,128)}, f32[80,640]{1,0:T(8,128)S(1)}, u32[]{:S(2)}) copy-start(f32[80,640]{1,0:T(8,128)S(1)} %collective-permute-done.3.refs_3_) | copy-start | bytes 614404
  28.3 10.7 %collective-permute-start.4 = (f32[80,640]{1,0:T(8,128)S(1)}, f32[80,640]{1,0:T(8,128)S(1)}, u32[]{:S(2)}, u32[]{:S(2)}) collective-permute-start(f32[80,640]{1,0:T(8,128)S(1)} %get-tuple-element.14), channel_id=1, source_target_pairs={{0,1},{1,2},{2,3},{3,4},{4,5},{5,6},{6,7},{7,8},{8,9},{9,10},{10,1... | collective-permute-start | bytes 614408 | tf_op jit(solution)/shard_map/ppermute | solution.py:21
  28.3 10.7 %copy-start.3 = (f32[80,640]{1,0:T(8,128)}, f32[80,640]{1,0:T(8,128)S(1)}, u32[]{:S(2)}) copy-start(f32[80,640]{1,0:T(8,128)S(1)} %collective-permute-done.2.refs_2_) | copy-start | bytes 614404
  28.3 10.7 %collective-permute-start.7 = (f32[80,640]{1,0:T(8,128)S(1)}, f32[80,640]{1,0:T(8,128)S(1)}, u32[]{:S(2)}, u32[]{:S(2)}) collective-permute-start(f32[80,640]{1,0:T(8,128)S(1)} %get-tuple-element.15), channel_id=1, source_target_pairs={{0,4},{1,5},{2,6},{3,7},{4,8},{5,9},{6,10},{7,11},{8,12},{9,13},{1... | collective-permute-start | bytes 614408 | tf_op jit(solution)/shard_map/ppermute | solution.py:21
  31.9 7.1 %copy-start.4 = (f32[80,640]{1,0:T(8,128)}, f32[80,640]{1,0:T(8,128)S(1)}, u32[]{:S(2)}) copy-start(f32[80,640]{1,0:T(8,128)S(1)} %collective-permute-done.1.refs_1_) | copy-start | bytes 614404
  31.9 7.1 %copy-start.5 = (f32[80,640]{1,0:T(8,128)}, f32[80,640]{1,0:T(8,128)S(1)}, u32[]{:S(2)}) copy-start(f32[80,640]{1,0:T(8,128)S(1)} %collective-permute-done.5.refs_5_) | copy-start | bytes 614404
  31.9 7.1 %copy-start.6 = (f32[80,640]{1,0:T(8,128)}, f32[80,640]{1,0:T(8,128)S(1)}, u32[]{:S(2)}) copy-start(f32[80,640]{1,0:T(8,128)S(1)} %collective-permute-done.refs_0_) | copy-start | bytes 614404
  39.0 0.7 copy-start.7
  39.7 0.7 copy-start.8
  83.8 7.1 %collective-permute-start.8 = (f32[24,160]{1,0:T(8,128)}, f32[24,160]{1,0:T(8,128)S(1)}, u32[]{:S(2)}, u32[]{:S(2)}) collective-permute-start(f32[24,160]{1,0:T(8,128)} %get-tuple-element.18), channel_id=1, source_target_pairs={{0,1},{1,2},{2,3},{3,4},{4,5},{5,6},{6,7},{7,8},{8,9},{9,10},{10,1... | collective-permute-start | bytes 46088 | tf_op jit(solution)/shard_map/ppermute | solution.py:21
  83.9 7.1 %collective-permute-start.9 = (f32[24,160]{1,0:T(8,128)}, f32[24,160]{1,0:T(8,128)S(1)}, u32[]{:S(2)}, u32[]{:S(2)}) collective-permute-start(f32[24,160]{1,0:T(8,128)} %get-tuple-element.19), channel_id=1, source_target_pairs={{0,31},{1,0},{2,1},{3,2},{4,3},{5,4},{6,5},{7,6},{8,7},{9,8},{10,9... | collective-permute-start | bytes 46088 | tf_op jit(solution)/shard_map/ppermute | solution.py:21
  91.7 5.8 %collective-permute-start.10 = (f32[8,160]{1,0:T(8,128)S(1)}, f32[8,160]{1,0:T(8,128)S(1)}, u32[]{:S(2)}, u32[]{:S(2)}) collective-permute-start(f32[8,160]{1,0:T(8,128)S(1)} %get-tuple-element.30), channel_id=1, source_target_pairs={{0,3},{1,4},{2,5},{3,6},{4,7},{5,8},{6,9},{7,10},{8,11},{9,12},{10... | collective-permute-start | bytes 15368 | tf_op jit(solution)/shard_map/ppermute | solution.py:21
  91.7 5.8 %collective-permute-start.11 = (f32[8,160]{1,0:T(8,128)S(1)}, f32[8,160]{1,0:T(8,128)S(1)}, u32[]{:S(2)}, u32[]{:S(2)}) collective-permute-start(f32[8,160]{1,0:T(8,128)S(1)} %get-tuple-element.31), channel_id=1, source_target_pairs={{0,29},{1,30},{2,31},{3,0},{4,1},{5,2},{6,3},{7,4},{8,5},{9,6},{10... | collective-permute-start | bytes 15368 | tf_op jit(solution)/shard_map/ppermute | solution.py:21

commit v3 on v2

--- a/solution.py
+++ b/solution.py
@@ -49,13 +49,13 @@
 
 
 def kernel(
-    ends, branches, core, request_row, request_col, deriv, *refs
+    place, ends, branches, core, request_row, request_col, deriv, *refs
 ):
     block_count = 2 * NB
     pieces = refs[:block_count]
-    density_out, own_out, near_up, near_down, far_up, far_down = refs[block_count : block_count + 6]
+    density_out, own_out, mail = refs[block_count : block_count + 3]
     (x, high_a, low_a, high_b, low_b, diag_row_a, diag_row_b, diag_col_a, diag_col_b, halo, density, deriv_held, row_part, deriv_sems, out_sem) = refs[
-        block_count + 6 :
+        block_count + 3 :
     ]
     rows, order = core.shape
     atoms = rows // ORB
@@ -215,24 +215,34 @@
     atom_ids = lax.broadcasted_iota(jnp.int32, (rows, atoms), 1)
     own_hot = (lax.broadcasted_iota(jnp.int32, (rows, atoms), 0) // ORB == atom_ids).astype(jnp.float32)
     own_out[...] = dot_one_hot(2.0 * (own_rows - columns[:, :rows]), own_hot.astype(jnp.bfloat16))
-    asked_hot = (request_col[...] == atom_ids).astype(jnp.float32).astype(jnp.bfloat16)
-    lane_block = lax.broadcasted_iota(jnp.int32, (8, order - rows), 1) // slot_rows
-    halo_columns = -2.0 * columns[:, rows:]
-    spread = jnp.concatenate(
-        [jnp.where(lane_block == block, halo_columns, 0.0) for block in range(block_count)], axis=0
-    )
-    terms = dot_one_hot(spread, asked_hot)
-    places = {
-        block_offset(block): terms[8 * block : 8 * block + 8, :] for block in range(block_count)
-    }
-    near_up[...] = jnp.concatenate([places[1], places[4], places[-2]], axis=0)
-    near_down[...] = jnp.concatenate([places[-1], places[-4], places[2]], axis=0)
-    far_up[...] = places[3]
-    far_down[...] = places[-3]
+    asked = request_row[...].astype(jnp.float32)
+    letter = jnp.where(line[:, rows:] == 3, asked, -2.0 * columns[:, rows:])
+    empty = jnp.where(lax.broadcasted_iota(jnp.int32, (4, SUB - slot_rows), 0) == 3, -1.0, 0.0)
+    mail[...] = jnp.zeros(mail.shape, jnp.float32)
+    for block in range(block_count):
+        content = letter[0:4, block * slot_rows : (block + 1) * slot_rows]
+        to = lax.rem(place[0] + (block_offset(block) + mail.shape[0]), mail.shape[0])
+        mail[to] = jnp.concatenate([content, empty], axis=1)
     out_copy.wait()
 
 
-def density_and_terms(ends, branches, core, request_row, request_col, deriv, pieces):
+def collect(place, mail, own, forces):
+    count = mail.shape[0]
+    atoms = own.shape[1]
+    letters = jnp.concatenate(
+        [mail[lax.rem(place[0] + (count - block_offset(block)), count)] for block in range(2 * NB)],
+        axis=1,
+    )
+    wanted = letters[3:4, :] == lax.broadcasted_iota(jnp.int32, (atoms, 1), 0).astype(jnp.float32)
+    wanted = wanted.astype(jnp.float32).astype(jnp.bfloat16)
+    sums = sum(
+        lax.dot_general(part, wanted, (((1,), (1,)), ((), ())), preferred_element_type=jnp.float32)
+        for part in thirds(jnp.concatenate([letters, letters], axis=0))
+    )
+    forces[...] = own[0:3, :] + sums[0:3, :]
+
+
+def density_and_terms(place, ends, branches, core, request_row, request_col, deriv, pieces):
     rows, order = core.shape
     atoms = rows // ORB
     block_count = len(pieces)
@@ -240,13 +250,15 @@
     smem = pl.BlockSpec(memory_space=pltpu.SMEM)
     anywhere = pl.BlockSpec(memory_space=pl.ANY)
     square = (order, order)
-    one = jax.ShapeDtypeStruct((8, atoms), jnp.float32)
-    three = jax.ShapeDtypeStruct((24, atoms), jnp.float32)
     return pl.pallas_call(
         kernel,
-        out_shape=[jax.ShapeDtypeStruct((rows, order), jnp.float32), one, three, three, one, one],
-        in_specs=[smem, smem, vmem, vmem, vmem, anywhere] + [vmem] * block_count,
-        out_specs=[anywhere] + [vmem] * 5,
+        out_shape=[
+            jax.ShapeDtypeStruct((rows, order), jnp.float32),
+            jax.ShapeDtypeStruct((8, atoms), jnp.float32),
+            jax.ShapeDtypeStruct((lax.axis_size("dom"), 4, SUB), jnp.float32),
+        ],
+        in_specs=[smem, smem, smem, vmem, vmem, vmem, anywhere] + [vmem] * block_count,
+        out_specs=[anywhere, vmem, vmem],
         scratch_shapes=[
             pltpu.VMEM(square, jnp.float32),
             pltpu.VMEM(square, jnp.bfloat16),
@@ -268,7 +280,7 @@
         cost_estimate=pl.CostEstimate(
             flops=2 * 3 * 3 * order**3, bytes_accessed=24_000_000, transcendentals=0
         ),
-    )(ends, branches, core, request_row, request_col, deriv, *pieces)
+    )(place, ends, branches, core, request_row, request_col, deriv, *pieces)
 
 
 def per_device(ham_core, halo_rows, halo_request, deriv, e_low, e_high, branches):
@@ -283,7 +295,9 @@
     for block, piece in zip(late, waiting):
         pieces[block] = passed_along(piece, "dom", -block_offset(block))
     request = jnp.repeat(halo_request[0], ORB)
-    density, forces, near_up, near_down, far_up, far_down = density_and_terms(
+    place = lax.axis_index("dom")[None].astype(jnp.int32)
+    density, own, mail = density_and_terms(
+        place,
         jnp.concatenate([e_high, e_low]),
         branches,
         ham_core,
@@ -292,13 +306,18 @@
         flat_deriv,
         [pieces[block] for block in range(block_count)],
     )
-    from_below = passed_along(near_up, "dom", 1)
-    from_above = passed_along(near_down, "dom", -1)
-    far_up = far_up + (from_below[8:16] + from_above[16:24])
-    far_down = far_down + (from_above[8:16] + from_below[16:24])
-    forces = forces + (from_below[:8] + from_above[:8])
-    forces = forces + (passed_along(far_up, "dom", 3) + passed_along(far_down, "dom", -3))
-    return (density, forces[:3])
+    arrived = lax.all_to_all(mail, "dom", 0, 0, tiled=True)
+    forces = pl.pallas_call(
+        collect,
+        out_shape=jax.ShapeDtypeStruct((3, own.shape[1]), jnp.float32),
+        in_specs=[
+            pl.BlockSpec(memory_space=pltpu.SMEM),
+            pl.BlockSpec(memory_space=pltpu.VMEM),
+            pl.BlockSpec(memory_space=pltpu.VMEM),
+        ],
+        out_specs=pl.BlockSpec(memory_space=pltpu.VMEM),
+    )(place, arrived, own)
+    return (density, forces)
 
 
 def solution(mesh):

time: 99.3 us -> 96 us (0.967)
  blocking collectives: 0 us -> 10.6 us
  starting transfers between devices: 23.6 us -> 13.8 us
  waiting for transfers between devices: 10.2 us -> 7.01 us
  other arithmetic: 2.61 us -> 0.64 us
  Pallas kernels: 43.5 us -> 45.1 us
    all_to_all x0 -> x1, blocking collectives: none -> 10.6 us  [per_device(): arrived = lax.all_to_all(mail, 'dom', 0, 0, tiled=True)]
    ppermute x12 -> x8, starting transfers between devices: 23.6 us -> 13.8 us  [passed_along(): return lax.ppermute(value, axis, pairs)]
    ppermute x12 -> x8, waiting for transfers between devices: 10.2 us -> 7.01 us  [passed_along(): return lax.ppermute(value, axis, pairs)]
    add x2 -> x0, other arithmetic: 2.01 us -> none  [the longest x1 1.29 us: per_device(): forces + (passed_along(far_up, 'dom', 3) + passed_along(far_down, 'dom',...]
    pallas_call x0 -> x1, Pallas kernels: none -> 1.83 us  [per_device(): pl.pallas_call(collect, out_shape=jax.ShapeDtypeStruct((3, own.shape[1]),...]
  transfers between devices with their start and end apart: 12 -> 8, of which waited for: 3 -> 1; matrix products, arithmetic and copies ran while one was open for 15% -> 15% of each run, Pallas kernels for 0% -> 0%
where the time goes in v3:
time: 96 us; the launch traced here: 95.5 us
  Pallas kernels  45.1 us (47%)
  local copies, waits for them, and re-layouts  16.2 us (17%)
  starting transfers between devices  13.8 us (14%)
  blocking collectives  10.6 us (11%)
  waiting for transfers between devices  7.01 us (7%)
  between operations  2.07 us (2%)
    pallas_call x1, Pallas kernels, density_and_terms(): pl.pallas_call(kernel, out_shape=[jax.ShapeDtypeStruct((rows, order), jnp...  43.3 us
    ppermute x8, starting transfers between devices, passed_along(): return lax.ppermute(value, axis, pairs)  13.8 us
    reshape x1, local copies, waits for them, and re-layouts, per_device(): flat_deriv = deriv.reshape(3, row_count, order_all)  12.3 us
    all_to_all x1, blocking collectives, per_device(): arrived = lax.all_to_all(mail, 'dom', 0, 0, tiled=True)  10.6 us
    ppermute x8, waiting for transfers between devices, passed_along(): return lax.ppermute(value, axis, pairs)  7.01 us
  transfers between devices with their start and end apart: 8, of which 1 were waited for; matrix products, arithmetic and copies ran while one was open for 15% of the time, Pallas kernels for 0%

profile of v3, /device:TPU:0, one launch (start us, length us, event | category | flops | bytes accessed | tf_op | source)
XLA Modules:
  0.0 95.5 jit_solution(18004783623247527656)
XLA Ops:
  0.6 1.6 %slice_bitcast_fusion = (f32[80,640]{1,0:T(8,128)S(1)}, f32[80,640]{1,0:T(8,128)S(1)}, f32[80,640]{1,0:T(8,128)S(1)}, f32[80,640]{1,0:T(8,128)S(1)}, f32[80,640]...) fusion(f32[1,8,80,1280]{3,2,1,0:T(8,128)} %param.8), kind=kLoop, calls=%fused_computation | loop fusion | bytes 3276800 | tf_op jit(solution)/shard_map/squeeze | solution.py:293
  2.2 2.4 %collective-permute-start.6 = (f32[80,640]{1,0:T(8,128)S(1)}, f32[80,640]{1,0:T(8,128)S(1)}, u32[]{:S(2)}, u32[]{:S(2)}) collective-permute-start(f32[80,640]{1,0:T(8,128)S(1)} %get-tuple-element.16), channel_id=1, source_target_pairs={{0,3},{1,4},{2,5},{3,6},{4,7},{5,8},{6,9},{7,10},{8,11},{9,12},{10... | collective-permute-start | bytes 614408 | tf_op jit(solution)/shard_map/ppermute | solution.py:21
  4.7 4.6 %collective-permute-start.3 = (f32[80,640]{1,0:T(8,128)S(1)}, f32[80,640]{1,0:T(8,128)S(1)}, u32[]{:S(2)}, u32[]{:S(2)}) collective-permute-start(f32[80,640]{1,0:T(8,128)S(1)} %get-tuple-element.17), channel_id=1, source_target_pairs={{0,28},{1,29},{2,30},{3,31},{4,0},{5,1},{6,2},{7,3},{8,4},{9,5},{1... | collective-permute-start | bytes 614408 | tf_op jit(solution)/shard_map/ppermute | solution.py:21
  9.2 0.5 collective-permute-start.2
  9.8 2.3 %collective-permute-start.1 = (f32[80,640]{1,0:T(8,128)S(1)}, f32[80,640]{1,0:T(8,128)S(1)}, u32[]{:S(2)}, u32[]{:S(2)}) collective-permute-start(f32[80,640]{1,0:T(8,128)S(1)} %get-tuple-element.19), channel_id=1, source_target_pairs={{0,30},{1,31},{2,0},{3,1},{4,2},{5,3},{6,4},{7,5},{8,6},{9,7},{10,... | collective-permute-start | bytes 614408 | tf_op jit(solution)/shard_map/ppermute | solution.py:21
  12.1 0.0 copy-start
  12.1 0.0 collective-permute-start.5
  12.1 12.3 %reshape.23.deriv = f32[3,640,1280]{2,1,0:T(8,128)} reshape(f32[3,160,4,1280]{3,2,1,0:T(4,128)} %param.10) | data formatting | bytes 19660800 | tf_op jit(solution)/shard_map/reshape | solution.py:290
  24.4 0.0 collective-permute-done.6.refs_6_
  24.4 0.0 copy-start.1
  24.4 3.9 %collective-permute-start = (f32[80,640]{1,0:T(8,128)S(1)}, f32[80,640]{1,0:T(8,128)S(1)}, u32[]{:S(2)}, u32[]{:S(2)}) collective-permute-start(f32[80,640]{1,0:T(8,128)S(1)} %get-tuple-element.10), channel_id=1, source_target_pairs={{0,31},{1,0},{2,1},{3,2},{4,3},{5,4},{6,5},{7,6},{8,7},{9,8},{10,9... | collective-permute-start | bytes 614408 | tf_op jit(solution)/shard_map/ppermute | solution.py:21
  28.3 0.0 collective-permute-done.3.refs_3_
  28.3 0.0 copy-start.2
  28.3 0.0 collective-permute-start.4
  28.3 0.0 collective-permute-done.2.refs_2_
  28.3 0.0 copy-start.3
  28.3 0.1 collective-permute-start.7
  28.4 0.0 copy-done
  28.4 0.1 broadcast_in_dim.7
  28.5 0.7 broadcast_in_dim_reshape.6.request_row
  29.2 0.9 broadcast_in_dim_reshape.8.request_col
  31.3 0.6 pad_maximum_fusion.ends
  32.0 0.0 collective-permute-done.1.refs_1_
  32.0 0.0 copy-start.4
  32.0 0.0 collective-permute-done.5.refs_5_
  32.0 0.0 copy-start.5
  32.0 0.0 collective-permute-done.refs_0_
  32.0 0.0 copy-start.6
  32.0 7.0 %collective-permute-done.4.refs_4_ = f32[80,640]{1,0:T(8,128)S(1)} collective-permute-done((f32[80,640]{1,0:T(8,128)S(1)}, f32[80,640]{1,0:T(8,128)S(1)}, u32[]{:S(2)}, u32[]{:S(2)}) %collective-permute-start.4) | collective-permute-done | bytes 204832 | tf_op jit(solution)/shard_map/ppermute | solution.py:21
  39.0 0.0 copy-start.7
  39.0 0.0 collective-permute-done.7.refs_7_
  39.0 0.0 copy-start.8
  39.0 0.0 copy-done.1
  39.0 0.0 copy-done.2
  39.0 0.0 copy-done.3
  39.0 0.0 copy-done.4
  39.1 0.0 copy-done.5
  39.1 0.0 copy-done.6
  39.1 0.6 copy-done.7
  39.7 0.1 copy-done.8
  39.8 43.3 %shard_map.86 = (f32[640,1280]{1,0:T(8,128)}, f32[8,160]{1,0:T(8,128)}, f32[32,4,128]{2,1,0:T(4,128)}) custom-call(s32[1]{0:T(128)} %bitcast.place, f32[2]{0:T(128)} %pad_maximum_fusion.ends, s32[5]{0:T(128)} %branches.1, f32[640,1280]{1,0:T(8,128)} %core.1, s32[1,640]{1,0:T(1,128)} %broadcast_in_dim_reshape.6.request_row, ...), custom_call_target="tpu_custom_call" | custom-call | flops 37748736000 | bytes 24000000 | tf_op jit(solution)/shard_map/pallas_call | solution.py:253
  83.1 10.6 %all_to_all.5.mail = f32[32,4,128]{2,1,0:T(4,128)} all-to-all(f32[32,4,128]{2,1,0:T(4,128)} %get-tuple-element.14), channel_id=1, replica_groups=mesh['dom'=32] {'dom'}, dimensions={0} | all-to-all | bytes 131072 | tf_op jit(solution)/shard_map/all_to_all | solution.py:309
  93.7 1.8 %shard_map.87 = f32[3,160]{1,0:T(4,128)} custom-call(s32[1]{0:T(128)} %bitcast.place, f32[32,4,128]{2,1,0:T(4,128)} %all_to_all.5.mail, f32[8,160]{1,0:T(8,128)} %get-tuple-element.15.own), custom_call_target="tpu_custom_call" | custom-call | tf_op jit(solution)/shard_map/pallas_call | solution.py:310
Async XLA Ops:
  2.2 22.2 %collective-permute-start.6 = (f32[80,640]{1,0:T(8,128)S(1)}, f32[80,640]{1,0:T(8,128)S(1)}, u32[]{:S(2)}, u32[]{:S(2)}) collective-permute-start(f32[80,640]{1,0:T(8,128)S(1)} %get-tuple-element.16), channel_id=1, source_target_pairs={{0,3},{1,4},{2,5},{3,6},{4,7},{5,8},{6,9},{7,10},{8,11},{9,12},{10... | collective-permute-start | bytes 614408 | tf_op jit(solution)/shard_map/ppermute | solution.py:21
  4.7 23.6 %collective-permute-start.3 = (f32[80,640]{1,0:T(8,128)S(1)}, f32[80,640]{1,0:T(8,128)S(1)}, u32[]{:S(2)}, u32[]{:S(2)}) collective-permute-start(f32[80,640]{1,0:T(8,128)S(1)} %get-tuple-element.17), channel_id=1, source_target_pairs={{0,28},{1,29},{2,30},{3,31},{4,0},{5,1},{6,2},{7,3},{8,4},{9,5},{1... | collective-permute-start | bytes 614408 | tf_op jit(solution)/shard_map/ppermute | solution.py:21
  9.2 19.1 %collective-permute-start.2 = (f32[80,640]{1,0:T(8,128)S(1)}, f32[80,640]{1,0:T(8,128)S(1)}, u32[]{:S(2)}, u32[]{:S(2)}) collective-permute-start(f32[80,640]{1,0:T(8,128)S(1)} %get-tuple-element.18), channel_id=1, source_target_pairs={{0,29},{1,30},{2,31},{3,0},{4,1},{5,2},{6,3},{7,4},{8,5},{9,6},{10... | collective-permute-start | bytes 614408 | tf_op jit(solution)/shard_map/ppermute | solution.py:21
  9.8 22.2 %collective-permute-start.1 = (f32[80,640]{1,0:T(8,128)S(1)}, f32[80,640]{1,0:T(8,128)S(1)}, u32[]{:S(2)}, u32[]{:S(2)}) collective-permute-start(f32[80,640]{1,0:T(8,128)S(1)} %get-tuple-element.19), channel_id=1, source_target_pairs={{0,30},{1,31},{2,0},{3,1},{4,2},{5,3},{6,4},{7,5},{8,6},{9,7},{10,... | collective-permute-start | bytes 614408 | tf_op jit(solution)/shard_map/ppermute | solution.py:21
  12.1 16.3 %copy-start = (s32[1,160]{1,0:T(1,128)S(1)}, s32[1,160]{1,0:T(1,128)}, u32[]{:S(2)}) copy-start(s32[1,160]{1,0:T(1,128)} %param.9) | copy-start | bytes 1924
  12.1 19.9 %collective-permute-start.5 = (f32[80,640]{1,0:T(8,128)S(1)}, f32[80,640]{1,0:T(8,128)S(1)}, u32[]{:S(2)}, u32[]{:S(2)}) collective-permute-start(f32[80,640]{1,0:T(8,128)S(1)} %get-tuple-element.23), channel_id=1, source_target_pairs={{0,2},{1,3},{2,4},{3,5},{4,6},{5,7},{6,8},{7,9},{8,10},{9,11},{10,... | collective-permute-start | bytes 614408 | tf_op jit(solution)/shard_map/ppermute | solution.py:21
  24.4 14.6 %copy-start.1 = (f32[80,640]{1,0:T(8,128)}, f32[80,640]{1,0:T(8,128)S(1)}, u32[]{:S(2)}) copy-start(f32[80,640]{1,0:T(8,128)S(1)} %collective-permute-done.6.refs_6_) | copy-start | bytes 614404
  24.4 7.6 %collective-permute-start = (f32[80,640]{1,0:T(8,128)S(1)}, f32[80,640]{1,0:T(8,128)S(1)}, u32[]{:S(2)}, u32[]{:S(2)}) collective-permute-start(f32[80,640]{1,0:T(8,128)S(1)} %get-tuple-element.10), channel_id=1, source_target_pairs={{0,31},{1,0},{2,1},{3,2},{4,3},{5,4},{6,5},{7,6},{8,7},{9,8},{10,9... | collective-permute-start | bytes 614408 | tf_op jit(solution)/shard_map/ppermute | solution.py:21
  28.3 10.7 %copy-start.2 = (f32[80,640]{1,0:T(8,128)}, f32[80,640]{1,0:T(8,128)S(1)}, u32[]{:S(2)}) copy-start(f32[80,640]{1,0:T(8,128)S(1)} %collective-permute-done.3.refs_3_) | copy-start | bytes 614404
  28.3 10.7 %collective-permute-start.4 = (f32[80,640]{1,0:T(8,128)S(1)}, f32[80,640]{1,0:T(8,128)S(1)}, u32[]{:S(2)}, u32[]{:S(2)}) collective-permute-start(f32[80,640]{1,0:T(8,128)S(1)} %get-tuple-element.11), channel_id=1, source_target_pairs={{0,1},{1,2},{2,3},{3,4},{4,5},{5,6},{6,7},{7,8},{8,9},{9,10},{10,1... | collective-permute-start | bytes 614408 | tf_op jit(solution)/shard_map/ppermute | solution.py:21
  28.3 10.7 %copy-start.3 = (f32[80,640]{1,0:T(8,128)}, f32[80,640]{1,0:T(8,128)S(1)}, u32[]{:S(2)}) copy-start(f32[80,640]{1,0:T(8,128)S(1)} %collective-permute-done.2.refs_2_) | copy-start | bytes 614404
  28.3 10.7 %collective-permute-start.7 = (f32[80,640]{1,0:T(8,128)S(1)}, f32[80,640]{1,0:T(8,128)S(1)}, u32[]{:S(2)}, u32[]{:S(2)}) collective-permute-start(f32[80,640]{1,0:T(8,128)S(1)} %get-tuple-element.12), channel_id=1, source_target_pairs={{0,4},{1,5},{2,6},{3,7},{4,8},{5,9},{6,10},{7,11},{8,12},{9,13},{1... | collective-permute-start | bytes 614408 | tf_op jit(solution)/shard_map/ppermute | solution.py:21
  32.0 7.1 %copy-start.4 = (f32[80,640]{1,0:T(8,128)}, f32[80,640]{1,0:T(8,128)S(1)}, u32[]{:S(2)}) copy-start(f32[80,640]{1,0:T(8,128)S(1)} %collective-permute-done.1.refs_1_) | copy-start | bytes 614404
  32.0 7.1 %copy-start.5 = (f32[80,640]{1,0:T(8,128)}, f32[80,640]{1,0:T(8,128)S(1)}, u32[]{:S(2)}) copy-start(f32[80,640]{1,0:T(8,128)S(1)} %collective-permute-done.5.refs_5_) | copy-start | bytes 614404
  32.0 7.1 %copy-start.6 = (f32[80,640]{1,0:T(8,128)}, f32[80,640]{1,0:T(8,128)S(1)}, u32[]{:S(2)}) copy-start(f32[80,640]{1,0:T(8,128)S(1)} %collective-permute-done.refs_0_) | copy-start | bytes 614404
  39.0 0.7 copy-start.7
  39.0 0.7 copy-start.8
